TPU v7x, 32 devices: a whole 2x2x4 slice. The times are simulated.
32 devices in a mesh: dp: 8 (over z, x), tensor: 4 (over y, core).
Axes of the slice: x: 2, y: 2, z: 4, core: 2. Of those that a mesh axis runs over, the one named last changes fastest.
Arguments:
- tokens: bfloat16 [32, 1024, 1024], P('dp', 'tensor'), may hold values from -6 to 6
- cotangent: bfloat16 [32, 1024, 1024], P('dp', 'tensor'), may hold values from -6 to 6
- destination: int32 [32], replicated, may hold values from 0 to 31, as said below
- lengths: int32 [32], replicated, may hold values from 128 to 1024, as said below
- adapter_of: int32 [32], replicated, may hold values from 0 to 7
- norm_gain: bfloat16 [1024], replicated, may hold values from 0.5 to 1.5
- w_zx: bfloat16 [1024, 2, 2048], P('dp', None, 'tensor'), may hold values from -0.1875 to 0.1875
- w_bc: bfloat16 [1024, 256], P('dp'), may hold values from -0.1875 to 0.1875
- w_dt: bfloat16 [1024, 32], P('dp', 'tensor'), may hold values from -0.1875 to 0.1875
- w_out: bfloat16 [1024, 2048], P('dp', 'tensor'), may hold values from -0.125 to 0.125
- conv_x: bfloat16 [5, 2048], P(None, 'tensor'), may hold values from -3 to 3
- conv_bc: bfloat16 [5, 256], replicated, may hold values from -3 to 3
- dt_bias: float32 [32], P('tensor'), may hold values from -7 to -2.5
- a_log: float32 [32], P('tensor'), may hold values from 0 to 2.77
- d_skip: float32 [32], P('tensor'), may hold values from 0.5 to 1.5
- out_gain: bfloat16 [2048], P('tensor'), may hold values from 0.5 to 1.5
- in_down: bfloat16 [1024, 128], replicated, may hold values from -0.1875 to 0.1875
- in_up: bfloat16 [128, 2, 2048], P(None, None, 'tensor'), may hold values from -1.5 to 1.5
- out_down: bfloat16 [128, 2048], replicated, may hold values from -0.125 to 0.125
- out_up: bfloat16 [128, 1024], replicated, may hold values from -1.5 to 1.5
Outputs:
- mixed: bfloat16 [32, 1024, 1024], P('dp', 'tensor')
- token_grad: bfloat16 [32, 1024, 1024], P('dp', 'tensor')
- in_down_grad: float32 [1024, 128], replicated
- in_up_grad: float32 [128, 2, 2048], P(None, None, 'tensor')
- out_down_grad: float32 [128, 2048], replicated
- out_up_grad: float32 [128, 1024], replicated
Inputs may be any that keep to these rules, and one draw needn't show every extreme that they name: `destination`: input sequence 4 * g + p goes to slot 4 * ((g + o[p]) mod 8) + p, with one offset o[p] for each position p of a group, the same for all groups. `lengths`: of the 4 sequences dealt to the slots of one data-shard group, one has length 1024.
All inputs are finite; a program needn't handle non-finite values.
Results may differ from a plain program's by a relative error of at most 0.0095.
Values may be sent and summed in bfloat16 or wider, within the bound.
No kernel may reach another device: no remote copies, remote signals or barrier semaphores. Data moves between devices by JAX's collectives and lax.ppermute only.
A program may use at most 256 MiB of HBM per device.

v0:
```python
import functools

import jax
import jax.numpy as jnp
from jax import lax
from jax.experimental import pallas as pl
from jax.experimental.pallas import tpu as pltpu
from jax.sharding import PartitionSpec as P

RANK = 16
SCAN = 128
ROWS = 256
TILE = 512
HEAD = 64
EPS = 1e-05
LIMIT = 58 * 1024 * 1024

f32 = jnp.float32
bf16 = jnp.bfloat16
ANY = pl.BlockSpec(memory_space=pl.ANY)
SMEM = pl.BlockSpec(memory_space=pltpu.SMEM)


def nn(a, b):
    return lax.dot_general(a, b, (((1,), (0,)), ((), ())), preferred_element_type=f32)


def nt(a, b):
    return lax.dot_general(a, b, (((1,), (1,)), ((), ())), preferred_element_type=f32)


def tn(a, b):
    return lax.dot_general(a, b, (((0,), (0,)), ((), ())), preferred_element_type=f32)


def exact(a, b):
    return lax.dot_general(
        a, b, (((1,), (0,)), ((), ())), preferred_element_type=f32, precision=lax.Precision.HIGHEST
    )


def halves(v, axis):
    high = v.astype(bf16)
    low = (v - high.astype(f32)).astype(bf16)
    return jnp.concatenate([high, low], axis=axis)


def sigmoid(v):
    return 1.0 / (1.0 + jnp.exp(-v))


def softplus(v):
    return jnp.maximum(v, 0.0) + jnp.log1p(jnp.exp(-jnp.abs(v)))


def triangle(n, lower):
    row = lax.broadcasted_iota(jnp.int32, (n, n), 0)
    col = lax.broadcasted_iota(jnp.int32, (n, n), 1)
    return row >= col if lower else row <= col


def head_vectors(vec, parts):
    width = vec.shape[1] // parts
    total = vec[8:16, 0:128]
    for t in range(1, parts):
        total = total + vec[8:16, t * width : t * width + 128]
    return total


def split_lanes(v):
    low_lanes = lax.broadcasted_iota(jnp.int32, v.shape, 1) < HEAD
    return jnp.where(low_lanes, v, 0.0).astype(bf16), jnp.where(low_lanes, 0.0, v).astype(bf16)


class Pieces:
    def __init__(self, arrays, moves):
        self.arrays, self.moves = arrays, moves


def copy_in(info, groups, sems):
    copies = []
    for refs, moves, full in groups:
        for which, index, take, place in moves:
            src = refs[which]
            if index is not None:
                src = src.at[index]
            if take is not None:
                src = src.at[take]
            copies.append(pltpu.make_async_copy(src, place(info, full), sems.at[len(copies)]))
    for copy in copies:
        copy.start()
    for copy in copies:
        copy.wait()


def whole_block(shape):
    return pl.BlockSpec(shape, lambda c: (0,) * len(shape))


def row_block(width, rows=ROWS):
    return pl.BlockSpec((rows, width), lambda c: (c, 0))


def take_refs(refs, counts):
    taken, at = [], 0
    for count in counts:
        taken.append(refs[at : at + count])
        at += count
    return taken, refs[at:]


def gathered_operands(names, pieces):
    owners, lists, arrays, counts = [], [], [], []
    for i, name in enumerate(names):
        owners.append(i if pieces[name].arrays else owners[-1])
        lists.append(pieces[name].moves)
        arrays += pieces[name].arrays
        counts.append(len(pieces[name].arrays))
    return (owners, lists), arrays, counts, sum(len(m) for m in lists)


def cost(micros):
    return pl.CostEstimate(flops=int(micros * 1.1e9), bytes_accessed=1 << 20, transcendentals=0)


def scan_kernel(names, moves, counts, parts, heads, *refs):
    info, gain, in_down, convbc, spread_heads = refs[:5]
    groups, rest = take_refs(refs[5:], counts)
    (x_out, w_full, bc_full, dt_full, vec, up, normed_out, low_out, pre_out, values_out, scanned_out) = rest[:11]
    (keys_out, prebc_out, scal_out, states_out, xs, dt_wide, xbuf, bcbuf, state, sems) = rest[11:]
    fulls = dict(x=xs, w=w_full, bc=bc_full, dt=dt_wide, vec=vec)
    c = pl.program_id(0)
    inner = w_full.shape[1]
    subs = ROWS // SCAN

    @pl.when(c == 0)
    def _():
        copy_in(info, [(groups[g], m, fulls[name]) for name, g, m in zip(names, moves[0], moves[1])], sems)
        state[...] = jnp.zeros_like(state)
        xbuf[0:8, :] = jnp.zeros((8, inner), f32)
        bcbuf[0:8, :] = jnp.zeros((8, bcbuf.shape[1]), f32)
        up[...] = vec[16 : 16 + RANK, :].astype(bf16)
        own = heads // parts
        dt_full[...] = jnp.concatenate(
            [dt_wide[16 * t : 16 * t + 16, :].astype(f32)[:own] for t in range(parts)], axis=0
        ).astype(bf16)

    x_low = xs[pl.ds(pl.multiple_of(c * ROWS, ROWS), ROWS), :]
    x_out[...] = x_low
    x = x_low.astype(f32)
    rms = lax.rsqrt(jnp.mean(x * x, axis=1, keepdims=True) + EPS)
    normed_out[...] = (x * rms * gain[...]).astype(bf16)
    low_out[...] = nn(normed_out[...], in_down[...]).astype(bf16)
    hv = head_vectors(vec, parts)
    bias, rate = hv[0:1, 0:heads], -jnp.exp(hv[1:2, 0:heads])

    bcbuf[8:, :] = nn(normed_out[...], bc_full[...])
    pre = convbc[4:5, :] + sum(convbc[k : k + 1, :] * bcbuf[5 + k : 5 + k + ROWS, :] for k in range(4))
    bcbuf[0:8, :] = bcbuf[ROWS : ROWS + 8, :]
    prebc_out[...] = pre
    keys_out[...] = (pre * sigmoid(pre)).astype(bf16)
    nstate = keys_out.shape[1] // 2

    raw = nt(normed_out[...], dt_full[...]) + bias
    steps = softplus(raw)
    lower = triangle(SCAN, True)
    lower_f = lower.astype(f32)
    cums, cum_rows, grown, scores, key_cols = [], [], [], [], []
    for s in range(subs):
        rows = slice(s * SCAN, (s + 1) * SCAN)
        dt_s = steps[rows]
        cum = exact(lower_f, dt_s * rate)
        cums.append(cum)
        cum_rows.append(cum.T)
        b_part, c_part = keys_out[rows, 0:nstate], keys_out[rows, nstate:]
        scores.append(jnp.where(lower, nt(c_part, b_part), 0.0))
        key_cols.append(b_part.astype(f32).T.astype(bf16))
        tail = jnp.exp(cum[SCAN - 1 : SCAN, :] - cum)
        grown.append((halves(dt_s, 1), halves(jnp.exp(cum), 1), halves(dt_s * tail, 1)))
    scal_out[...] = jnp.concatenate(
        [steps, jnp.concatenate(cums, axis=0), sigmoid(raw), jnp.zeros((ROWS, 128 - 3 * heads), f32)], axis=1
    )

    for j in range(inner // TILE):
        cols = slice(j * TILE, (j + 1) * TILE)
        xbuf[8:, cols] = nn(normed_out[...], w_full[:, cols]) + nn(low_out[...], up[:, cols])
        halo = xbuf[:, cols]
        pre = vec[4:5, cols] + vec[3:4, cols] * halo[8:]
        pre = pre + sum(vec[k : k + 1, cols] * pltpu.roll(halo, 3 - k, 0)[8:] for k in range(3))
        xbuf[0:8, cols] = xbuf[ROWS : ROWS + 8, cols]
        pre_out[:, cols] = pre.astype(bf16)
        values_out[:, cols] = (pre * sigmoid(pre)).astype(bf16)
        for s in range(subs):
            rows = slice(s * SCAN, (s + 1) * SCAN)
            dtx, ecx, tlx = (nn(v, spread_heads[:, cols]) for v in grown[s])
            state_low = state[:, cols].astype(bf16)
            states_out[s, :, cols] = state_low
            v = values_out[rows, cols].astype(f32)
            y = ecx * nn(keys_out[rows, nstate:], state_low) + vec[6:7, cols] * v
            vw = v * dtx
            within = []
            for p in range(TILE // 128):
                lhs = []
                for a in range(2):
                    h = (j * TILE + p * 128) // HEAD + a
                    gap = cums[s][:, h : h + 1] - cum_rows[s][h : h + 1, :]
                    lhs.append((jnp.exp(jnp.minimum(gap, 0.0)) * scores[s]).astype(bf16))
                rhs = jnp.concatenate(split_lanes(vw[:, p * 128 : (p + 1) * 128]), axis=0)
                within.append(nn(jnp.concatenate(lhs, axis=1), rhs))
            scanned_out[rows, cols] = y + jnp.concatenate(within, axis=1)
            state[:, cols] = ecx[SCAN - 1 : SCAN, :] * state[:, cols] + nn(key_cols[s], (v * tlx).astype(bf16))


def call_scan(info, gain, in_down, convbc, spread_heads, pieces, parts, heads, length, width, inner):
    names = ("x", "w", "bc", "dt", "vec")
    moves, arrays, counts, total = gathered_operands(names, pieces)
    two_n = convbc.shape[1]
    steps, subs = length // ROWS, ROWS // SCAN
    shapes = [
        ((length, width), bf16), ((width, inner), bf16), ((width, two_n), bf16), ((heads, width), bf16),
        ((16 + 2 * RANK, inner), f32), ((RANK, inner), bf16), ((length, width), bf16), ((length, RANK), bf16),
        ((length, inner), bf16), ((length, inner), bf16), ((length, inner), f32), ((length, two_n), bf16),
        ((length, two_n), f32), ((length, 128), f32), ((length // SCAN, two_n // 2, inner), bf16),
    ]
    specs = [
        row_block(width), whole_block((width, inner)), whole_block((width, two_n)), whole_block((heads, width)),
        whole_block((16 + 2 * RANK, inner)), whole_block((RANK, inner)), row_block(width), row_block(RANK),
        row_block(inner), row_block(inner), row_block(inner), row_block(two_n),
        row_block(two_n), row_block(128), pl.BlockSpec((subs, two_n // 2, inner), lambda c: (c, 0, 0)),
    ]
    return pl.pallas_call(
        functools.partial(scan_kernel, names, moves, counts, parts, heads),
        grid=(steps,),
        in_specs=[SMEM, whole_block(gain.shape), whole_block(in_down.shape), whole_block(convbc.shape)]
        + [whole_block(spread_heads.shape)] + [ANY] * len(arrays),
        out_shape=[jax.ShapeDtypeStruct(s, d) for s, d in shapes],
        out_specs=specs,
        scratch_shapes=[
            pltpu.VMEM((length, width), bf16), pltpu.VMEM((parts * 16, width), bf16),
            pltpu.VMEM((ROWS + 8, inner), f32), pltpu.VMEM((ROWS + 8, two_n), f32),
            pltpu.VMEM((two_n // 2, inner), f32), pltpu.SemaphoreType.DMA((total,)),
        ],
        compiler_params=pltpu.CompilerParams(vmem_limit_bytes=LIMIT, dimension_semantics=("arbitrary",)),
        cost_estimate=cost(44),
    )(info, gain, in_down, convbc, spread_heads, *arrays)


def gate_kernel(names, moves, counts, *refs):
    info, normed, low, scanned, x, vec, out_down, out_up = refs[:8]
    groups, rest = take_refs(refs[8:], counts)
    (mixed_out, dlayer_out, dy_out, side_out, back_out, low_back_out, in_up_out, out_down_out) = rest[:8]
    (wz, wo, upz, cots, z, gi, gated, gg, zg, sems) = rest[8:]
    fulls = dict(z=wz, o=wo, cot=cots)
    c = pl.program_id(0)
    inner = wz.shape[1]
    tiles = [slice(j * TILE, (j + 1) * TILE) for j in range(inner // TILE)]

    @pl.when(c == 0)
    def _():
        copy_in(info, [(groups[g], m, fulls[name]) for name, g, m in zip(names, moves[0], moves[1])], sems)
        upz[...] = vec[16 + RANK : 16 + 2 * RANK, :].astype(bf16)
        in_up_out[...] = jnp.zeros_like(in_up_out)
        out_down_out[...] = jnp.zeros_like(out_down_out)

    squares = jnp.zeros((ROWS, 128), f32)
    for cols in tiles:
        zj = nn(normed[...], wz[:, cols]) + nn(low[...], upz[:, cols])
        z[:, cols] = zj
        g = scanned[:, cols] * (zj * sigmoid(zj))
        gi[:, cols] = g
        g = g * g
        squares = squares + sum(g[:, k : k + 128] for k in range(0, TILE, 128))
    scale = lax.rsqrt(jnp.sum(squares, axis=1, keepdims=True) / inner + EPS)
    for cols in tiles:
        gated[:, cols] = (gi[:, cols] * scale * vec[5:6, cols]).astype(bf16)
    side = nt(gated[...], out_down[...]).astype(bf16)
    side_out[...] = side
    terms = nt(gated[...], wo[...]) + nn(side, out_up[...])
    live = lax.broadcasted_iota(jnp.int32, (ROWS, 1), 0) + c * ROWS < info[0]
    mixed = jnp.where(live, x[...].astype(f32) + terms, 0.0).astype(bf16)
    if len(mixed_out.shape) == 2:
        mixed_out[...] = mixed
    else:
        chunk = mixed_out.shape[2]
        for j in range(mixed_out.shape[0]):
            mixed_out[j, 0, :, :] = mixed[j * chunk : (j + 1) * chunk, :]
    cot = cots[pl.ds(pl.multiple_of(c * ROWS, ROWS), ROWS), :]
    dlayer_out[...] = jnp.where(live, cot.astype(f32), 0.0).astype(bf16)
    side_grad = nt(dlayer_out[...], out_up[...]).astype(bf16)
    products = jnp.zeros((ROWS, 128), f32)
    for cols in tiles:
        grad = (nn(dlayer_out[...], wo[:, cols]) + nn(side_grad, out_down[:, cols])).astype(bf16)
        gg[:, cols] = grad
        g = grad.astype(f32) * vec[5:6, cols] * gi[:, cols]
        products = products + sum(g[:, k : k + 128] for k in range(0, TILE, 128))
    factor = scale * scale * scale * (jnp.sum(products, axis=1, keepdims=True) / inner)
    for cols in tiles:
        grad = scale * (gg[:, cols].astype(f32) * vec[5:6, cols]) - gi[:, cols] * factor
        zj = z[:, cols]
        sig = sigmoid(zj)
        sc = scanned[:, cols].astype(f32)
        dy = (grad * (zj * sig)).astype(bf16)
        dy_out[:, cols] = dy
        zg[:, cols] = (grad * sc * (sig * (1.0 + zj * (1.0 - sig)))).astype(bf16)
    back_out[...] = nt(zg[...], wz[...])
    low_back_out[...] = nt(zg[...], upz[...])
    in_up_out[...] += tn(low[...], zg[...])
    out_down_out[...] += tn(side_grad, gated[...])


def call_gate(info, normed, low, scanned, x, vec, out_down, out_up, pieces, groups, parts):
    names = ("z", "o", "cot")
    moves, arrays, counts, total = gathered_operands(names, pieces)
    length, width = x.shape
    inner = scanned.shape[1]
    chunk = length // (groups * parts)
    if chunk % 16 == 0 and length // parts == ROWS:
        leaving = ((groups, parts, chunk, width), pl.BlockSpec((groups, 1, chunk, width), lambda c: (0, c, 0, 0)))
    else:
        leaving = ((length, width), row_block(width))
    shapes = [
        (leaving[0], bf16), ((length, width), bf16), ((length, inner), bf16), ((length, RANK), bf16),
        ((length, width), f32), ((length, RANK), f32), ((RANK, inner), f32), ((RANK, inner), f32),
    ]
    specs = [
        leaving[1], row_block(width), row_block(inner), row_block(RANK), row_block(width), row_block(RANK),
        whole_block((RANK, inner)), whole_block((RANK, inner)),
    ]
    return pl.pallas_call(
        functools.partial(gate_kernel, names, moves, counts),
        grid=(length // ROWS,),
        in_specs=[SMEM, row_block(width), row_block(RANK), row_block(inner), row_block(width), whole_block(vec.shape)]
        + [whole_block(out_down.shape), whole_block(out_up.shape)] + [ANY] * len(arrays),
        out_shape=[jax.ShapeDtypeStruct(s, d) for s, d in shapes],
        out_specs=specs,
        scratch_shapes=[
            pltpu.VMEM((width, inner), bf16), pltpu.VMEM((width, inner), bf16), pltpu.VMEM((RANK, inner), bf16),
            pltpu.VMEM((length, width), bf16), pltpu.VMEM((ROWS, inner), f32), pltpu.VMEM((ROWS, inner), f32),
            pltpu.VMEM((ROWS, inner), bf16), pltpu.VMEM((ROWS, inner), bf16), pltpu.VMEM((ROWS, inner), bf16),
            pltpu.SemaphoreType.DMA((total,)),
        ],
        compiler_params=pltpu.CompilerParams(vmem_limit_bytes=LIMIT, dimension_semantics=("arbitrary",)),
        cost_estimate=cost(43),
    )(info, normed, low, scanned, x, vec, out_down, out_up, *arrays)


def back_kernel(groups, parts, heads, *refs):
    (x, normed, low, dlayer, dy, values, pre, keys, prebc, scal, states, scanned, side, back, low_back) = refs[:15]
    (w_full, bc_full, dt_full, vec, up, gain, in_down, convbc, spread_heads, head_sum) = refs[15:25]
    (in_up_z, out_down, grad_out) = refs[25:28]
    outs, (in_up_x, out_up, in_down_sum, dstate, xbuf, bcbuf, xg, summed) = refs[28:-8], refs[-8:]
    i = pl.program_id(0)
    inner = w_full.shape[1]
    subs = ROWS // SCAN
    nstate = keys.shape[1] // 2
    tiles = [slice(j * TILE, (j + 1) * TILE) for j in range(inner // TILE)]

    @pl.when(i == 0)
    def _():
        dstate[...] = jnp.zeros_like(dstate)
        xbuf[ROWS:, :] = jnp.zeros((8, inner), f32)
        bcbuf[ROWS:, :] = jnp.zeros((8, bcbuf.shape[1]), f32)
        summed[...] = jnp.zeros_like(summed)
        for total in (in_up_x, out_up, in_down_sum):
            total[...] = jnp.zeros_like(total)

    hv = head_vectors(vec, parts)
    rate = -jnp.exp(hv[1:2, 0:heads])
    upper = triangle(SCAN, False)
    upper_f = upper.astype(f32)
    raw_parts = [None] * subs
    for s in reversed(range(subs)):
        rows = slice(s * SCAN, (s + 1) * SCAN)
        steps, cum = scal[rows, 0:heads], scal[rows, heads : 2 * heads]
        cum_row = cum.T
        last = cum[SCAN - 1 : SCAN, :]
        dt2, ecum2, tail2 = halves(steps, 1), halves(jnp.exp(cum), 1), halves(jnp.exp(last - cum), 1)
        b_part, c_part = keys[rows, 0:nstate], keys[rows, nstate:]
        c_cols = c_part.astype(f32).T.astype(bf16)
        scores = jnp.where(upper, nt(b_part, c_part), 0.0)
        pulled = jnp.zeros((SCAN, SCAN), f32)
        c_grad = jnp.zeros((SCAN, nstate), f32)
        b_grad = jnp.zeros((SCAN, nstate), f32)
        direct = jnp.zeros((SCAN, heads), f32)
        change = jnp.zeros((SCAN, heads), f32)
        for j, cols in enumerate(tiles):
            dtx, ecx, tlx = (nn(v, spread_heads[:, cols]) for v in (dt2, ecum2, tail2))
            g_low = dy[rows, cols]
            g = g_low.astype(f32)
            v = values[rows, cols].astype(f32)
            vw = v * dtx
            dstate_low = dstate[:, cols].astype(bf16)
            within = []
            for p in range(TILE // 128):
                part = slice(p * 128, (p + 1) * 128)
                vw_split = split_lanes(vw[:, part])
                lhs = []
                for a in range(2):
                    h = (j * TILE + p * 128) // HEAD + a
                    gap = cum_row[h : h + 1, :] - cum[:, h : h + 1]
                    decay = jnp.exp(jnp.minimum(gap, 0.0))
                    pulled = pulled + decay * nt(vw_split[a], g_low[:, part])
                    lhs.append((decay * scores).astype(bf16))
                rhs = jnp.concatenate(split_lanes(g[:, part]), axis=0)
                within.append(nn(jnp.concatenate(lhs, axis=1), rhs))
            dvw = jnp.concatenate(within, axis=1) + tlx * nn(b_part, dstate_low)
            vg = dtx * dvw + vec[6:7, cols] * g
            summer = head_sum[cols, :]
            direct = direct + nn((v * dvw).astype(bf16), summer)
            summer = jnp.concatenate([summer, summer], axis=0)
            change = change + nn(halves(g * scanned[rows, cols] - v * vg, 1), summer)
            ge = (ecx * g).astype(bf16)
            c_grad = c_grad + nt(ge, states[s, :, cols])
            b_grad = b_grad + nt((tlx * vw).astype(bf16), dstate_low)
            dstate[:, cols] = ecx[SCAN - 1 : SCAN, :] * dstate[:, cols] + nn(c_cols, ge)
            pv = pre[rows, cols].astype(f32)
            sig = sigmoid(pv)
            xbuf[rows, cols] = vg * (sig * (1.0 + pv * (1.0 - sig)))
        pulled = jnp.where(upper, pulled, 0.0)
        b_grad = b_grad + nn(pulled.astype(bf16), c_part)
        c_grad = c_grad + nn(pulled.T.astype(bf16), b_part)
        pb = prebc[rows, :]
        sig = sigmoid(pb)
        bcbuf[rows, :] = jnp.concatenate([b_grad, c_grad], axis=1) * (sig * (1.0 + pb * (1.0 - sig)))
        later = exact(upper_f, change) + summed[0:1, 0:heads]
        summed[0:1, 0:heads] = later[0:1, :]
        raw_parts[s] = (direct + rate * later) * scal[rows, 2 * heads : 3 * heads]
    raw_grad = jnp.concatenate(raw_parts, axis=0).astype(bf16)

    for cols in tiles:
        halo = xbuf[:, cols]
        total = vec[3:4, cols] * halo[:ROWS]
        total = total + sum(vec[k : k + 1, cols] * pltpu.roll(halo, ROWS + 5 + k, 0)[:ROWS] for k in range(3))
        xg[:, cols] = total.astype(bf16)
    xbuf[ROWS:, :] = xbuf[0:8, :]
    bc_grad = sum(convbc[k : k + 1, :] * bcbuf[3 - k : 3 - k + ROWS, :] for k in range(4)).astype(bf16)
    bcbuf[ROWS:, :] = bcbuf[0:8, :]
    low_grad = (low_back[...] + nt(xg[...], up[...])).astype(bf16)
    in_up_x[...] += tn(low[...], xg[...])
    out_up[...] += tn(side[...], dlayer[...])
    in_down_sum[...] += tn(low_grad, normed[...])
    ng = back[...] + nt(xg[...], w_full[...]) + nt(bc_grad, bc_full[...])
    ng = ng + nn(raw_grad, dt_full[...]) + nt(low_grad, in_down[...])
    xv = x[...].astype(f32)
    rms = lax.rsqrt(jnp.mean(xv * xv, axis=1, keepdims=True) + EPS)
    ng = ng * gain[...]
    inner_norm = jnp.mean(ng * xv, axis=1, keepdims=True)
    grad_out[...] = (dlayer[...].astype(f32) + rms * ng - xv * (rms * rms * rms * inner_norm)).astype(bf16)


    @pl.when(i == pl.num_programs(0) - 1)
    def _():
        if len(outs) > 1:
            for out, total in zip(outs, (in_up_z, in_up_x, out_up, in_down_sum)):
                out[...] = total[...].astype(bf16)
            return
        (shares,) = outs
        cols = inner // parts
        for g in range(groups):
            for t in range(parts):
                own = g * parts + t
                at = g * 2 * cols // groups
                total = in_up_z if at < cols else in_up_x
                at = at % cols + t * cols
                wide = 2 * cols // groups
                shares[own, :, 0:wide] = total[:, at : at + wide].astype(bf16)
                other = shares.shape[2] - wide
                at = own * other
                for total in (out_down, out_up, in_down_sum):
                    if 0 <= at < total.shape[1]:
                        shares[own, :, wide:] = total[:, at : at + other].astype(bf16)
                    at = at - total.shape[1]


def shares_of(groups, parts, inner, width):
    ups, others = 2 * inner // (groups * parts), (inner + 2 * width) // (groups * parts)
    return None if ups % 128 or others % 128 or width % others or inner % others else ups + others


def call_back(rows_in, consts, groups, parts, heads):
    x = rows_in[0]
    length, width = x.shape
    inner = rows_in[4].shape[1]
    two_n = rows_in[7].shape[1]
    steps, subs = length // ROWS, ROWS // SCAN
    shares = shares_of(groups, parts, inner, width)
    if shares is None:
        sums = [(RANK, inner), (RANK, inner), (RANK, width), (RANK, width)]
    else:
        sums = [(groups * parts, RANK, shares)]

    def spec(a):
        if a.ndim == 3:
            return pl.BlockSpec((subs,) + a.shape[1:], lambda i: (steps - 1 - i, 0, 0))
        return pl.BlockSpec((ROWS, a.shape[1]), lambda i: (steps - 1 - i, 0))

    return pl.pallas_call(
        functools.partial(back_kernel, groups, parts, heads),
        grid=(steps,),
        in_specs=[spec(a) for a in rows_in] + [whole_block(a.shape) for a in consts],
        out_shape=[jax.ShapeDtypeStruct((length, width), bf16)] + [jax.ShapeDtypeStruct(s, bf16) for s in sums],
        out_specs=[spec(x)] + [whole_block(s) for s in sums],
        scratch_shapes=[
            pltpu.VMEM((RANK, inner), f32), pltpu.VMEM((RANK, width), f32), pltpu.VMEM((RANK, width), f32),
            pltpu.VMEM((two_n // 2, inner), f32),
            pltpu.VMEM((ROWS + 8, inner), f32), pltpu.VMEM((ROWS + 8, two_n), f32), pltpu.VMEM((ROWS, inner), bf16),
            pltpu.VMEM((8, 128), f32),
        ],
        compiler_params=pltpu.CompilerParams(vmem_limit_bytes=LIMIT, dimension_semantics=("arbitrary",)),
        cost_estimate=cost(50),
    )(*rows_in, *consts)


def turn_kernel(info, came, leave):
    groups, parts = came.shape[:2]
    for p in range(parts):
        for d in range(groups):
            leave[d, p, :, :] = came[lax.rem(d + groups - info[p], groups), p, :, :]


def call_turn(offsets, came):
    return pl.pallas_call(
        turn_kernel,
        in_specs=[SMEM, pl.BlockSpec(memory_space=pltpu.VMEM)],
        out_shape=jax.ShapeDtypeStruct(came.shape, came.dtype),
        out_specs=pl.BlockSpec(memory_space=pltpu.VMEM),
        compiler_params=pltpu.CompilerParams(vmem_limit_bytes=LIMIT),
        cost_estimate=cost(3),
    )(offsets, came)


def arrange_kernel(labels, far_labels, groups, parts, info, sums, *refs):
    far, (in_up, out_down, out_up, in_down) = refs[:-4], refs[-4:]
    cols = in_up.shape[1] // groups
    for i, label in enumerate(labels):
        g = info[1 + label["z"] * 2 + label["x"]]
        in_up[:, lanes(g, cols)] = sums[i, :, 0:cols].astype(f32)
    width = far[0].shape[2]
    first, second = out_down.shape[1] // width, out_up.shape[1] // width
    at = 0
    for part in far:
        for i in range(part.shape[0]):
            label = far_labels[at]
            at += 1
            own = info[1 + label["z"] * 2 + label["x"]] * parts + info[1 + groups + label["y"] * 2 + label["c"]]

            @pl.when(own < first)
            def _():
                out_down[:, lanes(own, width)] = part[i, :, :].astype(f32)

            @pl.when((own >= first) & (own < first + second))
            def _():
                out_up[:, lanes(own - first, width)] = part[i, :, :].astype(f32)

            @pl.when(own >= first + second)
            def _():
                in_down[lanes(own - first - second, width), :] = part[i, :, :].astype(f32).T


def call_arrange(info, sums, far_sums, labels, far_labels, groups, parts, inner, width, cols):
    rows = sums.shape[1]
    vmem = pl.BlockSpec(memory_space=pltpu.VMEM)
    shapes = [(rows, 2 * cols), (rows, inner), (rows, width), (width, rows)]
    return pl.pallas_call(
        functools.partial(arrange_kernel, labels, far_labels, groups, parts),
        in_specs=[SMEM, vmem] + [vmem] * len(far_sums),
        out_shape=[jax.ShapeDtypeStruct(s, f32) for s in shapes],
        out_specs=[vmem] * 4,
        compiler_params=pltpu.CompilerParams(vmem_limit_bytes=LIMIT),
        cost_estimate=cost(3),
    )(info, sums, *far_sums)


def moved(block, axis, route):
    size = lax.axis_size(axis)
    return lax.ppermute(block, axis, [(i, route(i, size)) for i in range(size)])


def hop(name, block):
    axis = "dp" if name in "zx" else "tensor"
    if name in "xc":
        return [moved(block, axis, lambda i, n: i ^ 1)]
    return [
        moved(block, axis, functools.partial(lambda k, i, n: (i + 2 * k) % n, k))
        for k in range(1, lax.axis_size(axis) // 2)
    ]


def widened(name, block, labels):
    got = hop(name, block)
    lists = labels + sum([[dict(label, **{name: k + 1}) for label in labels] for k in range(len(got))], [])
    return [block] + got, lists


HERE = dict(z=0, x=0, y=0, c=0)


def tie(first, *others):
    return lax.optimization_barrier((first,) + others)[0]


def index_table(length_of, groups, parts, group, rank):
    dp_from = [((group ^ kx) - 2 * kz) % groups for kz in range(groups // 2) for kx in range(2)]
    part_from = [((rank ^ kc) - 2 * ky) % parts for ky in range(parts // 2) for kc in range(2)]
    partner = [rank ^ k for k in range(parts)]
    return jnp.stack([length_of] + dp_from + part_from + partner).astype(jnp.int32)


def placed(arrays, labels, groups, take, place):
    moves, at = [], 0
    for which, array in enumerate(arrays):
        for index in range(array.shape[0]):
            label = labels[at]
            at += 1
            if label is None:
                continue
            g_at = 1 + label["z"] * 2 + label["x"]
            t_at = 1 + groups + label["y"] * 2 + label["c"]
            moves.append((which, index, take, functools.partial(
                lambda g_at, t_at, info, full: place(info[g_at], info[t_at], full), g_at, t_at)))
    return Pieces(list(arrays), moves)


def paired(arrays, groups, parts, index, place):
    moves = [
        (k, index, None, functools.partial(lambda at, info, full: place(info[at], full), 1 + groups + parts + k))
        for k in range(parts)
    ]
    return Pieces(list(arrays), moves)


def single(array):
    return Pieces([array], [(0, None, None, lambda info, full: full)])


def span(index, size, offset=0, step=None):
    return pl.ds(pl.multiple_of(index * (size if step is None else step) + offset, 16), size)


def lanes(index, size):
    return pl.ds(pl.multiple_of(index * size, size), size)


def exchanged(blocks):
    return [
        block if k == 0 else moved(block, "tensor", functools.partial(lambda k, i, n: i ^ k, k))
        for k, block in enumerate(blocks)
    ]


def on_device(
    tokens, cotangent, destination, lengths, adapter_of, norm_gain, w_zx, w_bc, w_dt, w_out,
    conv_x, conv_bc, dt_bias, a_log, d_skip, out_gain, in_down, in_up, out_down, out_up,
):
    groups, parts = lax.axis_size("dp"), lax.axis_size("tensor")
    group, rank = lax.axis_index("dp"), lax.axis_index("tensor")
    seq_grp, part_len, width = tokens.shape
    rows, _, cols = w_zx.shape
    own_heads = w_dt.shape[1]
    length, inner, heads = part_len * parts, cols * parts, own_heads * parts
    mine = group * seq_grp + rank
    offset = destination[rank] // seq_grp
    adapter = adapter_of[mine] * RANK
    info = index_table(lengths[mine], groups, parts, group, rank)

    def swapped(array, axes="tensor"):
        return lax.all_to_all(array, axes, split_axis=0, concat_axis=0, tiled=True)

    def col_place(t, full):
        return full.at[:, lanes(t, cols)]

    down_in = lax.dynamic_slice_in_dim(in_down, adapter, RANK, 1)
    down_out = lax.dynamic_slice_in_dim(out_down, adapter, RANK, 0)
    up_out = lax.dynamic_slice_in_dim(out_up, adapter, RANK, 0)
    gain = norm_gain.astype(f32)[None]
    convbc = jnp.pad(conv_bc.astype(f32), ((0, 3), (0, 0)))
    head_of = jnp.arange(inner) // (inner // heads)
    spread_heads = (jnp.arange(2 * heads)[:, None] % heads == head_of[None, :]).astype(bf16)
    small_inputs = (info, down_in, gain, convbc, spread_heads)

    head_rows = lax.dynamic_update_slice(jnp.zeros((8, cols), f32), jnp.stack([dt_bias, a_log]), (0, rank * own_heads))
    own_vec = jnp.concatenate([
        conv_x.astype(f32), out_gain.astype(f32)[None], jnp.repeat(d_skip, cols // own_heads)[None],
        jnp.zeros((1, cols), f32), head_rows])

    half, share, two_n = rows // 2, rows // parts, w_bc.shape[1]
    packed = share % 32 == 0 and rows % 128 == 0 and cols == 2 * two_n
    w_x = w_zx[:, 1]
    if packed:
        own_bc = lax.dynamic_slice_in_dim(w_bc, rank * share, share, 0)
        own_bc = jnp.concatenate([own_bc[: share // 2], own_bc[share // 2 :]], axis=1)
        own_dt = jnp.zeros((16, cols), bf16).at[:own_heads, :rows].set(w_dt.T)
        block = jnp.concatenate([w_x[:half], own_bc, w_x[half:], own_dt])
    else:
        block = w_x
    extra = block.shape[0] // 2
    along_z, labels = widened("z", jnp.concatenate([block, w_out])[None], [HERE])
    wz, wz_labels = widened("y", w_zx[:, 0][None], [HERE])
    along_z, wz, token_rows = lax.optimization_barrier((along_z, wz, swapped(tokens)))

    own_vec, in_up = lax.optimization_barrier((own_vec, in_up, along_z))[:2]
    vecs = []
    for k in range(parts):
        theirs = lax.dynamic_slice_in_dim(in_up, adapter_of[group * seq_grp + k] * RANK, RANK, 0)
        vecs.append(jnp.concatenate([own_vec, theirs[:, 1].astype(f32), theirs[:, 0].astype(f32)]))

    first, first_labels = widened("x", jnp.concatenate([a[:, :extra] for a in along_z]), labels)
    second, second_labels = widened("y", jnp.concatenate([a[:, extra : 2 * extra] for a in along_z]), labels)
    wo, wo_labels = jnp.concatenate([a[:, 2 * extra :] for a in along_z]), labels
    wz, wz_labels = widened("z", jnp.concatenate(wz), wz_labels)
    first, second, wz[1], wz[-1], wo, vecs = lax.optimization_barrier((first, second, wz[1], wz[-1], wo, jnp.stack(vecs)))

    vec_rows = swapped(vecs)
    near = len(wz_labels) // len(wz)
    wz_near = jnp.concatenate([wz[0], wz[1], wz[-1]]) if len(wz) > 2 else jnp.concatenate(wz)
    near_labels = wz_labels[: 2 * near] + (wz_labels[-near:] if len(wz) > 2 else [])
    first = jnp.concatenate(first)
    second = jnp.concatenate(second)
    gathered = [first, second] + hop("c", first) + hop("c", second)
    first, far_first_labels = widened("y", first, first_labels)
    second, far_second_labels = widened("x", second, second_labels)
    wz_far, far_labels = wz[2:-1], wz_labels[2 * near : -near]
    first, second, wz_far, wz_near, vec_rows, gathered, small_inputs = lax.optimization_barrier(
        (first[1:], second[1:], wz_far, wz_near, vec_rows, gathered, small_inputs)
    )
    info, down_in, gain, convbc, spread_heads = small_inputs

    both_labels = [first_labels, second_labels]
    both_labels += [[dict(label, c=1) for label in labels] for labels in both_labels]
    halves_of = [0, 1, 0, 1]
    for which, arrays, labels, own in ((0, first, far_first_labels, first_labels), (1, second, far_second_labels, second_labels)):
        labels = labels[len(own) :]
        for at, array in enumerate(arrays):
            part = labels[at * len(own) : (at + 1) * len(own)]
            gathered += [array] + hop("c", array)
            both_labels += [part, [dict(label, c=1) for label in part]]
            halves_of += [which, which]
    x_pieces = single(token_rows.reshape(length, width))
    vec_pieces = Pieces([vec_rows], [
        (0, k, None, functools.partial(lambda k, info, full: full.at[:, pl.ds(k * cols, cols)], k)) for k in range(parts)])

    def of_half(which):
        return sum([labels if which == h else [None] * len(labels) for labels, h in zip(both_labels, halves_of)], [])

    x_weights = placed(
        gathered, of_half(0), groups, (pl.ds(0, half),),
        lambda g, t, full: full.at[span(g, half, 0, rows), lanes(t, cols)],
    )
    x_weights.moves += placed(
        gathered, of_half(1), groups, (pl.ds(0, half),),
        lambda g, t, full: full.at[span(g, half, half, rows), lanes(t, cols)],
    ).moves
    if packed:
        bc_weights = placed(
            gathered, of_half(0), groups, (pl.ds(half, 16), pl.ds(0, two_n)),
            lambda g, t, full: full.at[span(g * parts + t, 16, 0, share), :],
        )
        bc_weights.moves += placed(
            gathered, of_half(0), groups, (pl.ds(half, 16), pl.ds(two_n, two_n)),
            lambda g, t, full: full.at[span(g * parts + t, 16, 16, share), :],
        ).moves
        dt_weights = placed(
            gathered, of_half(1), groups, (pl.ds(half, 16), pl.ds(0, rows)),
            lambda g, t, full: full.at[span(t, 16), lanes(g, rows)],
        )
        bc_weights.arrays, dt_weights.arrays = [], []
    else:
        bc_weights = single(lax.all_gather(w_bc, "dp", axis=0, tiled=True))
        all_dt = lax.all_gather(lax.all_gather(w_dt, "dp", axis=0, tiled=True), "tensor", axis=0)
        all_dt = jnp.pad(all_dt.transpose(0, 2, 1), ((0, 0), (0, 16 - own_heads), (0, 0)))
        dt_weights = single(all_dt.reshape(parts * 16, width))

    wz, wz_labels = widened("x", wz_near, near_labels)
    for at, array in enumerate(wz_far):
        got, labels = widened("x", array, far_labels[at * near : (at + 1) * near])
        wz, wz_labels = wz + got, wz_labels + labels
    by_chip = [(wo, wo_labels), (hop("x", wo)[0], [dict(label, x=1) for label in wo_labels])]
    for k, got in enumerate(hop("y", wo)):
        by_chip.append((got, [dict(label, y=k + 1) for label in wo_labels]))
    for k in range(1, parts // 2):
        got = lax.ppermute(wo, ("dp", "tensor"), [
            (g * parts + t, (g ^ 1) * parts + (t + 2 * k) % parts) for g in range(groups) for t in range(parts)])
        by_chip.append((got, [dict(label, x=1, y=k) for label in wo_labels]))
    wo, wo_labels = [a for a, _ in by_chip], sum([lab for _, lab in by_chip], [])

    def block_place(g, t, full):
        return full.at[span(g, rows), lanes(t, cols)]

    def across_cores(arrays, labels):
        arrays = arrays + [hop("c", a)[0] for a in arrays]
        return placed(arrays, labels + [dict(label, c=1) for label in labels], groups, None, block_place)

    head_sum = (head_of[:, None] == jnp.arange(heads)[None, :]).astype(bf16)

    (x, w_full, bc_full, dt_full, vec, up, normed, low, pre, values, scanned, keys, prebc, scal, states) = call_scan(
        info, gain, down_in, convbc, spread_heads,
        dict(x=x_pieces, w=x_weights, bc=bc_weights, dt=dt_weights, vec=vec_pieces),
        parts, heads, length, width, inner,
    )

    cot_rows = swapped(tie(cotangent, gathered[0]))
    wz, wo, cot_rows, low = lax.optimization_barrier((wz, wo, cot_rows, low))
    cot_pieces = single(cot_rows.reshape(length, width))
    z_weights, o_weights = across_cores(wz, wz_labels), across_cores(wo, wo_labels)
    out = call_gate(
        info, normed, low, scanned, x, vec, down_out, up_out,
        dict(z=z_weights, o=o_weights, cot=cot_pieces), groups, parts,
    )
    mixed, dlayer, dy, side, back, low_back, up_z_part, out_down_part = out

    if mixed.ndim == 2:
        mixed = mixed.reshape(parts, groups, -1, width).transpose(1, 0, 2, 3)
    chunk = mixed.shape[2]
    came = swapped(mixed.reshape(groups * parts, chunk, width), ("dp", "tensor"))

    out = call_back(
        (x, normed, low, dlayer, dy, values, pre, keys, prebc, scal, states, scanned, side, back, low_back),
        (w_full, bc_full, dt_full, vec, up, gain, down_in, convbc, spread_heads, head_sum)
        + (up_z_part, out_down_part), groups, parts, heads,
    )
    came, out = lax.optimization_barrier((came, out))
    token_rows, sums = out[0], out[1:]

    offsets = destination[:seq_grp] // seq_grp
    leave = call_turn(offsets, came.reshape(groups, parts, chunk, width))

    def second_leg(leave):
        return swapped(leave, "dp").transpose(1, 0, 2, 3).reshape(parts, part_len, width)

    token_rows = token_rows.reshape(parts, part_len, width)
    token_grad = exchanged([lax.dynamic_index_in_dim(token_rows, rank ^ k, 0, keepdims=False) for k in range(parts)])

    def stacked(blocks):
        result = jnp.zeros((parts,) + blocks[0].shape, blocks[0].dtype)
        for k, block in enumerate(blocks):
            result = lax.dynamic_update_index_in_dim(result, block, rank ^ k, 0)
        return result

    own = groups * parts
    if len(sums) > 1:

        def at_adapter(part):
            zeros = jnp.zeros((in_down.shape[1], part.shape[1]), bf16)
            return lax.dynamic_update_slice_in_dim(zeros, part.astype(bf16), adapter, 0)

        in_up_grad = [lax.psum_scatter(at_adapter(a), "tensor", scatter_dimension=1, tiled=True) for a in sums[:2]]
        in_up_grad = lax.psum(jnp.stack(in_up_grad, axis=1), "dp").astype(f32)
        others = [at_adapter(a) for a in (out_down_part, sums[2], sums[3])]
        out_down_grad, out_up_grad, in_down_grad = (a.astype(f32) for a in lax.psum(others, ("dp", "tensor")))
        return second_leg(leave), stacked(token_grad), in_down_grad.T, in_up_grad, out_down_grad, out_up_grad

    pooled = swapped(sums[0], ("dp", "tensor"))
    row_of = adapter_of[:, None] * RANK + jnp.arange(RANK)[None, :]
    select = (row_of.reshape(1, -1) == jnp.arange(in_down.shape[1])[:, None]).astype(bf16)
    sums = nn(select, pooled.reshape(own * RANK, -1)).astype(bf16)[None]
    sums, labels = widened("z", sums, [HERE])
    sums, leave = lax.optimization_barrier((sums, leave))
    mixed = second_leg(leave)
    sums, labels = widened("x", jnp.concatenate(sums), labels)
    sums = jnp.concatenate(sums)
    far_sums, far_labels = widened("y", sums[:, :, 2 * cols // groups :], labels)
    far_sums, token_grad = lax.optimization_barrier((jnp.concatenate(far_sums), token_grad))
    far_sums, far_labels = widened("c", far_sums, far_labels)
    in_up_grad, out_down_grad, out_up_grad, in_down_grad = call_arrange(
        info, sums, far_sums, labels, far_labels, groups, parts, inner, width, cols
    )
    in_up_grad = jnp.stack([in_up_grad[:, :cols], in_up_grad[:, cols:]], axis=1)
    return (mixed, stacked(token_grad), in_down_grad, in_up_grad, out_down_grad, out_up_grad)


def solution(mesh):
    return jax.shard_map(
        on_device,
        mesh=mesh,
        in_specs=(
            P("dp", "tensor", None), P("dp", "tensor", None), P(), P(), P(), P(),
            P("dp", None, "tensor"), P("dp", None), P("dp", "tensor"), P("dp", "tensor"),
            P(None, "tensor"), P(), P("tensor"), P("tensor"), P("tensor"), P("tensor"),
            P(), P(None, None, "tensor"), P(), P(),
        ),
        out_specs=(
            P("dp", "tensor", None), P("dp", "tensor", None), P(), P(None, None, "tensor"), P(), P(),
        ),
        check_vma=False,
    )
```

profile of v0, /device:TPU:0, one launch (start us, length us, event | category | flops | bytes accessed | tf_op | source)
XLA Modules:
  0.0 305.1 jit_solution(11492250944504516411)
XLA Ops:
  0.7 4.4 %all-to-all-start = ((bf16[4,256,1024]{2,1,0:T(8,128)(2,1)}), bf16[4,256,1024]{2,1,0:T(8,128)(2,1)S(1)}, u32[]{:S(2)}, u32[]{:S(2)}) async-start(bf16[4,256,1024]{2,1,0:T(8,128)(2,1)} %param.22), calls=%async_computation | async-start | bytes 4194304 | tf_op jit(solution)/shard_map/all_to_all | solution.py:667
  6.2 2.5 collective-permute-start
  8.7 2.6 collective-permute-start.1
  18.6 15.0 %collective-permute-done.3 = bf16[1,128,512]{2,1,0:T(8,128)(2,1)S(1)} collective-permute-done((bf16[1,128,512]{2,1,0:T(8,128)(2,1)S(1)}, bf16[1,128,512]{2,1,0:T(8,128)(2,1)S(1)}, u32[]{:S(2)}, u32[]{:S(2)}) %collective-permute-start.3) | collective-permute-done | bytes 131104 | tf_op jit(solution)/shard_map/ppermute | solution.py:576
  35.1 4.3 %collective-permute-start.6 = (bf16[2,128,512]{2,1,0:T(8,128)(2,1)}, bf16[2,128,512]{2,1,0:T(8,128)(2,1)S(1)}, u32[]{:S(2)}, u32[]{:S(2)}) collective-permute-start(bf16[2,128,512]{2,1,0:T(8,128)(2,1)} %constant_dynamic-update-slice_fusion.3), channel_id=1, source_target_pairs={{0,8},{4,12},{8,16},{12,20},{16,24},{20,28},{24,0},{28,4},{1,9},{5... | collective-permute-start | bytes 786440 | tf_op jit(solution)/shard_map/ppermute | solution.py:576
  59.4 3.5 %all-to-all-start.1 = ((f32[4,48,512]{2,1,0:T(8,128)}), f32[4,48,512]{2,1,0:T(8,128)S(1)}, u32[]{:S(2)}, u32[]{:S(2)}) async-start(f32[4,48,512]{2,1,0:T(8,128)} %pad_maximum_fusion.4), calls=%async_computation.1 | async-start | bytes 786432 | tf_op jit(solution)/shard_map/all_to_all | solution.py:667
  67.7 6.0 %collective-permute-done.10.refs_10_ = bf16[2,128,512]{2,1,0:T(8,128)(2,1)} collective-permute-done((bf16[2,128,512]{2,1,0:T(8,128)(2,1)}, bf16[2,128,512]{2,1,0:T(8,128)(2,1)}, u32[]{:S(2)}, u32[]{:S(2)}) %collective-permute-start.10) | collective-permute-done | bytes 262176 | tf_op jit(solution)/shard_map/ppermute | solution.py:576
  73.7 4.8 %all-to-all-done.1.refs_14_ = f32[4,48,512]{2,1,0:T(8,128)S(1)} async-done(((f32[4,48,512]{2,1,0:T(8,128)}), f32[4,48,512]{2,1,0:T(8,128)S(1)}, u32[]{:S(2)}, u32[]{:S(2)}) %all-to-all-start.1) | async-done | bytes 393248 | tf_op jit(solution)/shard_map/all_to_all | solution.py:667
  80.4 2.2 collective-permute-start.19
  82.6 3.8 %all-to-all-start.2 = ((bf16[4,256,1024]{2,1,0:T(8,128)(2,1)}), bf16[4,256,1024]{2,1,0:T(8,128)(2,1)S(1)}, u32[]{:S(2)}, u32[]{:S(2)}) async-start(bf16[4,256,1024]{2,1,0:T(8,128)(2,1)} %param.23), calls=%async_computation.2 | async-start | bytes 4194304 | tf_op jit(solution)/shard_map/all_to_all | solution.py:667
  88.5 35.8 %shard_map.235 = (bf16[1024,1024]{1,0:T(8,128)(2,1)}, bf16[1024,2048]{1,0:T(8,128)(2,1)}, bf16[1024,256]{1,0:T(8,128)(2,1)}, bf16[32,1024]{1,0:T(8,128)(2,1)}, f...) custom-call(s32[17]{0:T(128)} %stack.108.refs_0_.info, ...), custom_call_target="tpu_custom_call" | custom-call | flops 48399998976 | bytes 1048576 | tf_op jit(solution)/shard_map/pallas_call | solution.py:231
  124.3 2.7 collective-permute-done.16.refs_11_
  136.8 39.7 %shard_map.236 = (bf16[8,4,32,1024]{3,2,1,0:T(8,128)(2,1)}, bf16[1024,1024]{1,0:T(8,128)(2,1)}, bf16[1024,2048]{1,0:T(8,128)(2,1)}, bf16[1024,16]{1,0:T(8,128)(2...) custom-call(s32[17]{0:T(128)} %stack.108.refs_0_.info, ...), custom_call_target="tpu_custom_call" | custom-call | flops 47300001792 | bytes 1048576 | tf_op jit(solution)/shard_map/pallas_call | solution.py:329
  176.6 3.7 %all-to-all-start.3 = ((bf16[32,32,1024]{2,1,0:T(8,128)(2,1)}), bf16[32,32,1024]{2,1,0:T(8,128)(2,1)S(1)}, u32[]{:S(2)}, u32[]{:S(2)}) async-start(bf16[32,32,1024]{2,1,0:T(8,128)(2,1)} %bitcast.122), calls=%async_computation.3 | async-start | bytes 4194304 | tf_op jit(solution)/shard_map/all_to_all | solution.py:667
  180.3 42.8 %shard_map.237 = (bf16[1024,1024]{1,0:T(8,128)(2,1)}, bf16[32,16,256]{2,1,0:T(8,128)(2,1)}) custom-call(bf16[1024,1024]{1,0:T(8,128)(2,1)} %get-tuple-element.138.refs_4_.refs_0_, bf16[1024,1024]{1,0:T(8,128)(2,1)} %get-tuple-element.130.refs_1_, bf16[1024,16]{1,0:T(8,128)(2,1)} %get-tuple-element.136.refs_2_, ...), custom_call_target="tpu_custom_call" | custom-call | flops 54999998464 | bytes 1048576 | tf_op jit(solution)/shard_map/pallas_call | solution.py:497
  223.1 5.7 %all-to-all-done.3 = bf16[32,32,1024]{2,1,0:T(8,128)(2,1)S(1)} async-done(((bf16[32,32,1024]{2,1,0:T(8,128)(2,1)}), bf16[32,32,1024]{2,1,0:T(8,128)(2,1)S(1)}, u32[]{:S(2)}, u32[]{:S(2)}) %all-to-all-start.3) | async-done | bytes 2097184 | tf_op jit(solution)/shard_map/all_to_all | solution.py:667
  228.8 4.1 %all-to-all-start.4 = ((bf16[32,16,256]{2,1,0:T(8,128)(2,1)}), bf16[32,16,256]{2,1,0:T(8,128)(2,1)S(1)}, u32[]{:S(2)}, u32[]{:S(2)}) async-start(bf16[32,16,256]{2,1,0:T(8,128)(2,1)} %get-tuple-element.169), calls=%async_computation.4 | async-start | bytes 524288 | tf_op jit(solution)/shard_map/all_to_all | solution.py:667
  233.6 9.9 %all-to-all-done.4 = bf16[32,16,256]{2,1,0:T(8,128)(2,1)S(1)} async-done(((bf16[32,16,256]{2,1,0:T(8,128)(2,1)}), bf16[32,16,256]{2,1,0:T(8,128)(2,1)S(1)}, u32[]{:S(2)}, u32[]{:S(2)}) %all-to-all-start.4) | async-done | bytes 262176 | tf_op jit(solution)/shard_map/all_to_all | solution.py:667
  247.6 3.1 %shard_map.238 = bf16[8,4,32,1024]{3,2,1,0:T(8,128)(2,1)} custom-call(s32[4]{0:T(128)} %and_select_fusion.info, bf16[8,4,32,1024]{3,2,1,0:T(8,128)(2,1)} %bitcast.121), custom_call_target="tpu_custom_call" | custom-call | flops 3300000000 | bytes 1048576 | tf_op jit(solution)/shard_map/pallas_call | solution.py:522
  252.3 3.6 %all-to-all-start.5 = ((bf16[8,4,32,1024]{3,2,1,0:T(8,128)(2,1)}), bf16[8,4,32,1024]{3,2,1,0:T(8,128)(2,1)S(1)}, u32[]{:S(2)}, u32[]{:S(2)}) async-start(bf16[8,4,32,1024]{3,2,1,0:T(8,128)(2,1)} %shard_map.238), calls=%async_computation.5 | async-start | bytes 4194304 | tf_op jit(solution)/shard_map/all_to_all | solution.py:667
  261.6 17.8 %collective-permute-done.31 = bf16[4,128,256]{2,1,0:T(8,128)(2,1)S(1)} collective-permute-done((bf16[4,128,256]{2,1,0:T(8,128)(2,1)S(1)}, bf16[4,128,256]{2,1,0:T(8,128)(2,1)S(1)}, u32[]{:S(2)}, u32[]{:S(2)}) %collective-permute-start.31) | collective-permute-done | bytes 262176 | tf_op jit(solution)/shard_map/ppermute | solution.py:576
  280.8 8.1 %collective-permute-done.32 = bf16[8,128,128]{2,1,0:T(8,128)(2,1)S(1)} collective-permute-done((bf16[8,128,128]{2,1,0:T(8,128)(2,1)S(1)}, bf16[8,128,128]{2,1,0:T(8,128)(2,1)S(1)}, u32[]{:S(2)}, u32[]{:S(2)}) %collective-permute-start.32) | collective-permute-done | bytes 262176 | tf_op jit(solution)/shard_map/ppermute | solution.py:576
  294.8 4.2 %shard_map.239 = (f32[128,1024]{1,0:T(8,128)}, f32[128,2048]{1,0:T(8,128)}, f32[128,1024]{1,0:T(8,128)}, f32[1024,128]{1,0:T(8,128)}) custom-call(s32[17]{0:T(128)} %stack.108.refs_0_.info, bf16[8,128,256]{2,1,0:T(8,128)(2,1)} %copy-done.16, bf16[16,128,128]{2,1,0:T(8,128)(2,1)} %copy-done.9, bf16[16,128,128]{2,1,0:T(8,128)(2,1)} %copy-done.35), custom_call_target="tpu_custom_call" | custom-call | flops 3300000000 | bytes 1048576 | tf_op jit(solution)/shard_map/pallas_call | solution.py:564
  301.3 2.3 all-to-all-done.5
  (218 shorter events, 67.9 us)
Async XLA Ops:
  0.7 32.9 %all-to-all-start = ((bf16[4,256,1024]{2,1,0:T(8,128)(2,1)}), bf16[4,256,1024]{2,1,0:T(8,128)(2,1)S(1)}, u32[]{:S(2)}, u32[]{:S(2)}) async-start(bf16[4,256,1024]{2,1,0:T(8,128)(2,1)} %param.22), calls=%async_computation | async-start | bytes 4194304 | tf_op jit(solution)/shard_map/all_to_all | solution.py:667
  6.2 27.4 %collective-permute-start = (bf16[1,288,512]{2,1,0:T(8,128)(2,1)S(1)}, bf16[1,288,512]{2,1,0:T(8,128)(2,1)}, u32[]{:S(2)}, u32[]{:S(2)}) collective-permute-start(bf16[1,288,512]{2,1,0:T(8,128)(2,1)S(1)} %bitcast.130), channel_id=1, source_target_pairs={{0,8},{4,12},{8,16},{12,20},{16,24},{20,28},{24,0},{28,4},{1,9},{5... | collective-permute-start | bytes 884744 | tf_op jit(solution)/shard_map/ppermute | solution.py:576
  8.7 24.9 %collective-permute-start.1 = (bf16[1,288,512]{2,1,0:T(8,128)(2,1)S(1)}, bf16[1,288,512]{2,1,0:T(8,128)(2,1)}, u32[]{:S(2)}, u32[]{:S(2)}) collective-permute-start(bf16[1,288,512]{2,1,0:T(8,128)(2,1)S(1)} %bitcast.131), channel_id=1, source_target_pairs={{0,16},{4,20},{8,24},{12,28},{16,0},{20,4},{24,8},{28,12},{1,17},{... | collective-permute-start | bytes 884744 | tf_op jit(solution)/shard_map/ppermute | solution.py:576
  11.3 22.4 %collective-permute-start.2 = (bf16[1,288,512]{2,1,0:T(8,128)(2,1)S(1)}, bf16[1,288,512]{2,1,0:T(8,128)(2,1)}, u32[]{:S(2)}, u32[]{:S(2)}) collective-permute-start(bf16[1,288,512]{2,1,0:T(8,128)(2,1)S(1)} %bitcast.132), channel_id=1, source_target_pairs={{0,24},{4,28},{8,0},{12,4},{16,8},{20,12},{24,16},{28,20},{1,25},{... | collective-permute-start | bytes 884744 | tf_op jit(solution)/shard_map/ppermute | solution.py:576
  12.7 21.0 %collective-permute-start.3 = (bf16[1,128,512]{2,1,0:T(8,128)(2,1)S(1)}, bf16[1,128,512]{2,1,0:T(8,128)(2,1)S(1)}, u32[]{:S(2)}, u32[]{:S(2)}) collective-permute-start(bf16[1,128,512]{2,1,0:T(8,128)(2,1)S(1)} %bitcast.125), channel_id=1, source_target_pairs={{0,2},{1,3},{2,0},{3,1},{4,6},{5,7},{6,4},{7,5},{8,10},{9,11},{10,... | collective-permute-start | bytes 393224 | tf_op jit(solution)/shard_map/ppermute | solution.py:576
  35.1 16.2 %collective-permute-start.6 = (bf16[2,128,512]{2,1,0:T(8,128)(2,1)}, bf16[2,128,512]{2,1,0:T(8,128)(2,1)S(1)}, u32[]{:S(2)}, u32[]{:S(2)}) collective-permute-start(bf16[2,128,512]{2,1,0:T(8,128)(2,1)} %constant_dynamic-update-slice_fusion.3), channel_id=1, source_target_pairs={{0,8},{4,12},{8,16},{12,20},{16,24},{20,28},{24,0},{28,4},{1,9},{5... | collective-permute-start | bytes 786440 | tf_op jit(solution)/shard_map/ppermute | solution.py:576
  53.8 24.8 %collective-permute-start.12 = (bf16[8,80,512]{2,1,0:T(8,128)(2,1)S(1)}, bf16[8,80,512]{2,1,0:T(8,128)(2,1)}, u32[]{:S(2)}, u32[]{:S(2)}) collective-permute-start(bf16[8,80,512]{2,1,0:T(8,128)(2,1)S(1)} %constant_dynamic-update-slice_fusion.7.refs_7_), channel_id=1, source_target_pairs={{0,1},{1,0},{2,3},{3,2},{4,5},{5,4},{6,7},{7,6},{8,9},{9,8},{10,11... | collective-permute-start | bytes 1966088 | tf_op jit(solution)/shard_map/ppermute | solution.py:576
  53.8 24.7 %collective-permute-start.9 = (bf16[8,80,512]{2,1,0:T(8,128)(2,1)S(1)}, bf16[8,80,512]{2,1,0:T(8,128)(2,1)}, u32[]{:S(2)}, u32[]{:S(2)}) collective-permute-start(bf16[8,80,512]{2,1,0:T(8,128)(2,1)S(1)} %constant_dynamic-update-slice_fusion.7.refs_7_), channel_id=1, source_target_pairs={{0,4},{4,0},{8,12},{12,8},{16,20},{20,16},{24,28},{28,24},{1,5},{5... | collective-permute-start | bytes 1966088 | tf_op jit(solution)/shard_map/ppermute | solution.py:576
  57.0 21.6 %collective-permute-start.11 = (bf16[8,80,512]{2,1,0:T(8,128)(2,1)}, bf16[8,80,512]{2,1,0:T(8,128)(2,1)}, u32[]{:S(2)}, u32[]{:S(2)}) collective-permute-start(bf16[8,80,512]{2,1,0:T(8,128)(2,1)} %constant_dynamic-update-slice_fusion.5.refs_6_), channel_id=1, source_target_pairs={{0,1},{1,0},{2,3},{3,2},{4,5},{5,4},{6,7},{7,6},{8,9},{9,8},{10,11... | collective-permute-start | bytes 1966088 | tf_op jit(solution)/shard_map/ppermute | solution.py:576
  57.1 21.4 %collective-permute-start.8 = (bf16[8,80,512]{2,1,0:T(8,128)(2,1)}, bf16[8,80,512]{2,1,0:T(8,128)(2,1)}, u32[]{:S(2)}, u32[]{:S(2)}) collective-permute-start(bf16[8,80,512]{2,1,0:T(8,128)(2,1)} %constant_dynamic-update-slice_fusion.5.refs_6_), channel_id=1, source_target_pairs={{0,2},{1,3},{2,0},{3,1},{4,6},{5,7},{6,4},{7,5},{8,10},{9,11},{10,... | collective-permute-start | bytes 1966088 | tf_op jit(solution)/shard_map/ppermute | solution.py:576
  58.6 15.1 %collective-permute-start.10 = (bf16[2,128,512]{2,1,0:T(8,128)(2,1)}, bf16[2,128,512]{2,1,0:T(8,128)(2,1)}, u32[]{:S(2)}, u32[]{:S(2)}) collective-permute-start(bf16[2,128,512]{2,1,0:T(8,128)(2,1)} %constant_dynamic-update-slice_fusion.3), channel_id=1, source_target_pairs={{0,16},{4,20},{8,24},{12,28},{16,0},{20,4},{24,8},{28,12},{1,17},{... | collective-permute-start | bytes 786440 | tf_op jit(solution)/shard_map/ppermute | solution.py:576
  59.4 19.1 %all-to-all-start.1 = ((f32[4,48,512]{2,1,0:T(8,128)}), f32[4,48,512]{2,1,0:T(8,128)S(1)}, u32[]{:S(2)}, u32[]{:S(2)}) async-start(f32[4,48,512]{2,1,0:T(8,128)} %pad_maximum_fusion.4), calls=%async_computation.1 | async-start | bytes 786432 | tf_op jit(solution)/shard_map/all_to_all | solution.py:667
  79.1 45.2 %collective-permute-start.17 = (bf16[4,128,512]{2,1,0:T(8,128)(2,1)}, bf16[4,128,512]{2,1,0:T(8,128)(2,1)}, u32[]{:S(2)}, u32[]{:S(2)}) collective-permute-start(bf16[4,128,512]{2,1,0:T(8,128)(2,1)} %pad_maximum_fusion.1.refs_16_), channel_id=1, source_target_pairs={{0,4},{4,0},{8,12},{12,8},{16,20},{20,16},{24,28},{28,24},{1,5},{5... | collective-permute-start | bytes 1572872 | tf_op jit(solution)/shard_map/ppermute | solution.py:576
  79.7 44.6 %collective-permute-start.18 = (bf16[4,128,512]{2,1,0:T(8,128)(2,1)}, bf16[4,128,512]{2,1,0:T(8,128)(2,1)}, u32[]{:S(2)}, u32[]{:S(2)}) collective-permute-start(bf16[4,128,512]{2,1,0:T(8,128)(2,1)} %pad_maximum_fusion.1.refs_16_), channel_id=1, source_target_pairs={{0,2},{1,3},{2,0},{3,1},{4,6},{5,7},{6,4},{7,5},{8,10},{9,11},{10,... | collective-permute-start | bytes 1572872 | tf_op jit(solution)/shard_map/ppermute | solution.py:576
  80.4 43.9 %collective-permute-start.19 = (bf16[4,128,512]{2,1,0:T(8,128)(2,1)}, bf16[4,128,512]{2,1,0:T(8,128)(2,1)}, u32[]{:S(2)}, u32[]{:S(2)}) collective-permute-start(bf16[4,128,512]{2,1,0:T(8,128)(2,1)} %pad_maximum_fusion.1.refs_16_), channel_id=1, source_target_pairs={{0,6},{1,7},{2,4},{3,5},{4,2},{5,3},{6,0},{7,1},{8,14},{9,15},{10,... | collective-permute-start | bytes 1572872 | tf_op jit(solution)/shard_map/ppermute | solution.py:781
  82.6 45.1 %all-to-all-start.2 = ((bf16[4,256,1024]{2,1,0:T(8,128)(2,1)}), bf16[4,256,1024]{2,1,0:T(8,128)(2,1)S(1)}, u32[]{:S(2)}, u32[]{:S(2)}) async-start(bf16[4,256,1024]{2,1,0:T(8,128)(2,1)} %param.23), calls=%async_computation.2 | async-start | bytes 4194304 | tf_op jit(solution)/shard_map/all_to_all | solution.py:667
  86.4 41.3 %collective-permute-start.15 = (bf16[6,128,512]{2,1,0:T(8,128)(2,1)S(1)}, bf16[6,128,512]{2,1,0:T(8,128)(2,1)}, u32[]{:S(2)}, u32[]{:S(2)}) collective-permute-start(bf16[6,128,512]{2,1,0:T(8,128)(2,1)S(1)} %pad_maximum_fusion.refs_8_), channel_id=1, source_target_pairs={{0,4},{4,0},{8,12},{12,8},{16,20},{20,16},{24,28},{28,24},{1,5},{5... | collective-permute-start | bytes 2359304 | tf_op jit(solution)/shard_map/ppermute | solution.py:576
  87.0 40.0 %collective-permute-start.16 = (bf16[2,128,512]{2,1,0:T(8,128)(2,1)}, bf16[2,128,512]{2,1,0:T(8,128)(2,1)S(1)}, u32[]{:S(2)}, u32[]{:S(2)}) collective-permute-start(bf16[2,128,512]{2,1,0:T(8,128)(2,1)} %collective-permute-done.10.refs_10_), channel_id=1, source_target_pairs={{0,4},{4,0},{8,12},{12,8},{16,20},{20,16},{24,28},{28,24},{1,5},{5... | collective-permute-start | bytes 786440 | tf_op jit(solution)/shard_map/ppermute | solution.py:576
  176.6 52.2 %all-to-all-start.3 = ((bf16[32,32,1024]{2,1,0:T(8,128)(2,1)}), bf16[32,32,1024]{2,1,0:T(8,128)(2,1)S(1)}, u32[]{:S(2)}, u32[]{:S(2)}) async-start(bf16[32,32,1024]{2,1,0:T(8,128)(2,1)} %bitcast.122), calls=%async_computation.3 | async-start | bytes 4194304 | tf_op jit(solution)/shard_map/all_to_all | solution.py:667
  252.3 51.3 %all-to-all-start.5 = ((bf16[8,4,32,1024]{3,2,1,0:T(8,128)(2,1)}), bf16[8,4,32,1024]{3,2,1,0:T(8,128)(2,1)S(1)}, u32[]{:S(2)}, u32[]{:S(2)}) async-start(bf16[8,4,32,1024]{3,2,1,0:T(8,128)(2,1)} %shard_map.238), calls=%async_computation.5 | async-start | bytes 4194304 | tf_op jit(solution)/shard_map/all_to_all | solution.py:667
  257.6 31.3 %collective-permute-start.33 = (bf16[256,1024]{1,0:T(8,128)(2,1)S(1)}, bf16[256,1024]{1,0:T(8,128)(2,1)S(1)}, u32[]{:S(2)}, u32[]{:S(2)}) collective-permute-start(bf16[256,1024]{1,0:T(8,128)(2,1)S(1)} %get-tuple-element.200), channel_id=1, source_target_pairs={{0,1},{1,0},{2,3},{3,2},{4,5},{5,4},{6,7},{7,6},{8,9},{9,8},{10,11... | collective-permute-start | bytes 1572872 | tf_op jit(solution)/shard_map/ppermute | solution.py:576
  257.7 31.3 %collective-permute-start.34 = (bf16[256,1024]{1,0:T(8,128)(2,1)S(1)}, bf16[256,1024]{1,0:T(8,128)(2,1)S(1)}, u32[]{:S(2)}, u32[]{:S(2)}) collective-permute-start(bf16[256,1024]{1,0:T(8,128)(2,1)S(1)} %get-tuple-element.199), channel_id=1, source_target_pairs={{0,2},{1,3},{2,0},{3,1},{4,6},{5,7},{6,4},{7,5},{8,10},{9,11},{10,... | collective-permute-start | bytes 1572872 | tf_op jit(solution)/shard_map/ppermute | solution.py:576
  258.6 30.4 %collective-permute-start.35 = (bf16[256,1024]{1,0:T(8,128)(2,1)S(1)}, bf16[256,1024]{1,0:T(8,128)(2,1)S(1)}, u32[]{:S(2)}, u32[]{:S(2)}) collective-permute-start(bf16[256,1024]{1,0:T(8,128)(2,1)S(1)} %get-tuple-element.198), channel_id=1, source_target_pairs={{0,3},{1,2},{2,1},{3,0},{4,7},{5,6},{6,5},{7,4},{8,11},{9,10},{10,... | collective-permute-start | bytes 1572872 | tf_op jit(solution)/shard_map/ppermute | solution.py:576
  259.6 19.8 %collective-permute-start.31 = (bf16[4,128,256]{2,1,0:T(8,128)(2,1)S(1)}, bf16[4,128,256]{2,1,0:T(8,128)(2,1)S(1)}, u32[]{:S(2)}, u32[]{:S(2)}) collective-permute-start(bf16[4,128,256]{2,1,0:T(8,128)(2,1)S(1)} %pad_maximum_fusion.7), channel_id=1, source_target_pairs={{0,4},{4,0},{8,12},{12,8},{16,20},{20,16},{24,28},{28,24},{1,5},{5... | collective-permute-start | bytes 786440 | tf_op jit(solution)/shard_map/ppermute | solution.py:576
  (59 other events, 734.2 us)
where the time goes:
time: 306 us; the launch traced here: 305 us
  Pallas kernels  126 us (41%)
  waiting for transfers between devices  78.2 us (26%)
  starting transfers between devices  60.4 us (20%)
  local copies, waits for them, and re-layouts  30.3 us (10%)
  other arithmetic  5.71 us (2%)
  between operations  4.68 us (2%)
    ppermute x36, waiting for transfers between devices, moved(): return lax.ppermute(block, axis, [(i, route(i, size)) for i in range(size)])  55.6 us
    pallas_call x1, Pallas kernels, call_back(): pl.pallas_call(functools.partial(back_kernel, groups, parts, heads), grid...  42.8 us
    pallas_call x1, Pallas kernels, call_gate(): pl.pallas_call(functools.partial(gate_kernel, names, moves, counts), grid...  39.7 us
    pallas_call x1, Pallas kernels, call_scan(): pl.pallas_call(functools.partial(scan_kernel, names, moves, counts, parts...  35.8 us
    ppermute x36, starting transfers between devices, moved(): return lax.ppermute(block, axis, [(i, route(i, size)) for i in range(size)])  35.2 us
    all_to_all x6, starting transfers between devices, swapped(): return lax.all_to_all(array, axes, split_axis=0, concat_axis=0, tiled=True)  23 us
    all_to_all x6, waiting for transfers between devices, swapped(): return lax.all_to_all(array, axes, split_axis=0, concat_axis=0, tiled=True)  22.7 us
    unnamed x92, local copies, waits for them, and re-layouts  6.67 us
  transfers between devices with their start and end apart: 43, of which 15 were waited for; matrix products, arithmetic and copies ran while one was open for 10% of the time, Pallas kernels for 28%

commit v1 on v0

--- a/solution.py
+++ b/solution.py
@@ -126,9 +126,9 @@
 def scan_kernel(names, moves, counts, parts, heads, *refs):
     info, gain, in_down, convbc, spread_heads = refs[:5]
     groups, rest = take_refs(refs[5:], counts)
-    (x_out, w_full, bc_full, dt_full, vec, up, normed_out, low_out, pre_out, values_out, scanned_out) = rest[:11]
-    (keys_out, prebc_out, scal_out, states_out, xs, dt_wide, xbuf, bcbuf, state, sems) = rest[11:]
-    fulls = dict(x=xs, w=w_full, bc=bc_full, dt=dt_wide, vec=vec)
+    (x_out, w_full, bc_full, dt_full, vec, up, normed_out, low_out, slope_out, values_out, scanned_out) = rest[:11]
+    (keys_out, prebc_out, scal_out, states_out, vec_low, xs, dt_wide, xbuf, bcbuf, state, sems) = rest[11:]
+    fulls = dict(x=xs, w=w_full, bc=bc_full, dt=dt_wide, vec=vec_low)
     c = pl.program_id(0)
     inner = w_full.shape[1]
     subs = ROWS // SCAN
@@ -139,7 +139,11 @@
         state[...] = jnp.zeros_like(state)
         xbuf[0:8, :] = jnp.zeros((8, inner), f32)
         bcbuf[0:8, :] = jnp.zeros((8, bcbuf.shape[1]), f32)
-        up[...] = vec[16 : 16 + RANK, :].astype(bf16)
+        vec[16:, :] = vec_low[16:, :].astype(f32)
+        top = vec_low[0:16, :].astype(f32)
+        skip, bias, decay = (top[n : n + 1] + top[n + 1 : n + 2] + top[n + 2 : n + 3] for n in (6, 9, 12))
+        vec[0:16, :] = jnp.concatenate([top[0:6], skip, jnp.zeros_like(skip), bias, decay, jnp.zeros((6, inner), f32)], axis=0)
+        up[...] = vec_low[16 : 16 + RANK, :]
         own = heads // parts
         dt_full[...] = jnp.concatenate(
             [dt_wide[16 * t : 16 * t + 16, :].astype(f32)[:own] for t in range(parts)], axis=0
@@ -188,8 +192,9 @@
         pre = vec[4:5, cols] + vec[3:4, cols] * halo[8:]
         pre = pre + sum(vec[k : k + 1, cols] * pltpu.roll(halo, 3 - k, 0)[8:] for k in range(3))
         xbuf[0:8, cols] = xbuf[ROWS : ROWS + 8, cols]
-        pre_out[:, cols] = pre.astype(bf16)
-        values_out[:, cols] = (pre * sigmoid(pre)).astype(bf16)
+        sig = sigmoid(pre)
+        values_out[:, cols] = (pre * sig).astype(bf16)
+        slope_out[:, cols] = (sig * (1.0 + pre * (1.0 - sig))).astype(bf16)
         for s in range(subs):
             rows = slice(s * SCAN, (s + 1) * SCAN)
             dtx, ecx, tlx = (nn(v, spread_heads[:, cols]) for v in grown[s])
@@ -236,6 +241,7 @@
         out_shape=[jax.ShapeDtypeStruct(s, d) for s, d in shapes],
         out_specs=specs,
         scratch_shapes=[
+            pltpu.VMEM((16 + 2 * RANK, inner), bf16),
             pltpu.VMEM((length, width), bf16), pltpu.VMEM((parts * 16, width), bf16),
             pltpu.VMEM((ROWS + 8, inner), f32), pltpu.VMEM((ROWS + 8, two_n), f32),
             pltpu.VMEM((two_n // 2, inner), f32), pltpu.SemaphoreType.DMA((total,)),
@@ -248,8 +254,8 @@
 def gate_kernel(names, moves, counts, *refs):
     info, normed, low, scanned, x, vec, out_down, out_up = refs[:8]
     groups, rest = take_refs(refs[8:], counts)
-    (mixed_out, dlayer_out, dy_out, side_out, back_out, low_back_out, in_up_out, out_down_out) = rest[:8]
-    (wz, wo, upz, cots, z, gi, gated, gg, zg, sems) = rest[8:]
+    (mixed_out, dlayer_out, dy_out, side_out, zg, low_back_out, in_up_out, out_down_out, wz) = rest[:9]
+    (wo, upz, cots, z, gi, gated, gg, sems) = rest[9:]
     fulls = dict(z=wz, o=wo, cot=cots)
     c = pl.program_id(0)
     inner = wz.shape[1]
@@ -302,7 +308,6 @@
         dy = (grad * (zj * sig)).astype(bf16)
         dy_out[:, cols] = dy
         zg[:, cols] = (grad * sc * (sig * (1.0 + zj * (1.0 - sig)))).astype(bf16)
-    back_out[...] = nt(zg[...], wz[...])
     low_back_out[...] = nt(zg[...], upz[...])
     in_up_out[...] += tn(low[...], zg[...])
     out_down_out[...] += tn(side_grad, gated[...])
@@ -320,11 +325,12 @@
         leaving = ((length, width), row_block(width))
     shapes = [
         (leaving[0], bf16), ((length, width), bf16), ((length, inner), bf16), ((length, RANK), bf16),
-        ((length, width), f32), ((length, RANK), f32), ((RANK, inner), f32), ((RANK, inner), f32),
+        ((length, inner), bf16), ((length, RANK), f32), ((RANK, inner), f32), ((RANK, inner), f32),
+        ((width, inner), bf16),
     ]
     specs = [
-        leaving[1], row_block(width), row_block(inner), row_block(RANK), row_block(width), row_block(RANK),
-        whole_block((RANK, inner)), whole_block((RANK, inner)),
+        leaving[1], row_block(width), row_block(inner), row_block(RANK), row_block(inner), row_block(RANK),
+        whole_block((RANK, inner)), whole_block((RANK, inner)), whole_block((width, inner)),
     ]
     return pl.pallas_call(
         functools.partial(gate_kernel, names, moves, counts),
@@ -334,10 +340,9 @@
         out_shape=[jax.ShapeDtypeStruct(s, d) for s, d in shapes],
         out_specs=specs,
         scratch_shapes=[
-            pltpu.VMEM((width, inner), bf16), pltpu.VMEM((width, inner), bf16), pltpu.VMEM((RANK, inner), bf16),
-            pltpu.VMEM((length, width), bf16), pltpu.VMEM((ROWS, inner), f32), pltpu.VMEM((ROWS, inner), f32),
-            pltpu.VMEM((ROWS, inner), bf16), pltpu.VMEM((ROWS, inner), bf16), pltpu.VMEM((ROWS, inner), bf16),
-            pltpu.SemaphoreType.DMA((total,)),
+            pltpu.VMEM((width, inner), bf16), pltpu.VMEM((RANK, inner), bf16), pltpu.VMEM((length, width), bf16),
+            pltpu.VMEM((ROWS, inner), f32), pltpu.VMEM((ROWS, inner), f32), pltpu.VMEM((ROWS, inner), bf16),
+            pltpu.VMEM((ROWS, inner), bf16), pltpu.SemaphoreType.DMA((total,)),
         ],
         compiler_params=pltpu.CompilerParams(vmem_limit_bytes=LIMIT, dimension_semantics=("arbitrary",)),
         cost_estimate=cost(43),
@@ -345,10 +350,10 @@
 
 
 def back_kernel(groups, parts, heads, *refs):
-    (x, normed, low, dlayer, dy, values, pre, keys, prebc, scal, states, scanned, side, back, low_back) = refs[:15]
-    (w_full, bc_full, dt_full, vec, up, gain, in_down, convbc, spread_heads, head_sum) = refs[15:25]
-    (in_up_z, out_down, grad_out) = refs[25:28]
-    outs, (in_up_x, out_up, in_down_sum, dstate, xbuf, bcbuf, xg, summed) = refs[28:-8], refs[-8:]
+    (x, normed, low, dlayer, dy, values, slope, keys, prebc, scal, states, scanned, side, zg, low_back) = refs[:15]
+    (w_full, wz, bc_full, dt_full, vec, up, gain, in_down, convbc, spread_heads, head_sum) = refs[15:26]
+    (in_up_z, out_down, grad_out) = refs[26:29]
+    outs, (in_up_x, out_up, in_down_sum, dstate, xbuf, bcbuf, xg, summed) = refs[29:-8], refs[-8:]
     i = pl.program_id(0)
     inner = w_full.shape[1]
     subs = ROWS // SCAN
@@ -413,9 +418,7 @@
             c_grad = c_grad + nt(ge, states[s, :, cols])
             b_grad = b_grad + nt((tlx * vw).astype(bf16), dstate_low)
             dstate[:, cols] = ecx[SCAN - 1 : SCAN, :] * dstate[:, cols] + nn(c_cols, ge)
-            pv = pre[rows, cols].astype(f32)
-            sig = sigmoid(pv)
-            xbuf[rows, cols] = vg * (sig * (1.0 + pv * (1.0 - sig)))
+            xbuf[rows, cols] = vg * slope[rows, cols].astype(f32)
         pulled = jnp.where(upper, pulled, 0.0)
         b_grad = b_grad + nn(pulled.astype(bf16), c_part)
         c_grad = c_grad + nn(pulled.T.astype(bf16), b_part)
@@ -439,7 +442,7 @@
     in_up_x[...] += tn(low[...], xg[...])
     out_up[...] += tn(side[...], dlayer[...])
     in_down_sum[...] += tn(low_grad, normed[...])
-    ng = back[...] + nt(xg[...], w_full[...]) + nt(bc_grad, bc_full[...])
+    ng = nt(zg[...], wz[...]) + nt(xg[...], w_full[...]) + nt(bc_grad, bc_full[...])
     ng = ng + nn(raw_grad, dt_full[...]) + nt(low_grad, in_down[...])
     xv = x[...].astype(f32)
     rms = lax.rsqrt(jnp.mean(xv * xv, axis=1, keepdims=True) + EPS)
@@ -678,10 +681,13 @@
     spread_heads = (jnp.arange(2 * heads)[:, None] % heads == head_of[None, :]).astype(bf16)
     small_inputs = (info, down_in, gain, convbc, spread_heads)
 
-    head_rows = lax.dynamic_update_slice(jnp.zeros((8, cols), f32), jnp.stack([dt_bias, a_log]), (0, rank * own_heads))
+    head_rows = lax.dynamic_update_slice(jnp.zeros((2, cols), f32), jnp.stack([dt_bias, a_log]), (0, rank * own_heads))
+    exact_rows = jnp.concatenate([jnp.repeat(d_skip, cols // own_heads)[None], head_rows])
+    high = lax.reduce_precision(exact_rows, 8, 7)
+    middle = lax.reduce_precision(exact_rows - high, 8, 7)
+    thirds = jnp.stack([high, middle, exact_rows - high - middle], axis=1).astype(bf16).reshape(9, cols)
     own_vec = jnp.concatenate([
-        conv_x.astype(f32), out_gain.astype(f32)[None], jnp.repeat(d_skip, cols // own_heads)[None],
-        jnp.zeros((1, cols), f32), head_rows])
+        conv_x, out_gain[None], thirds, jnp.zeros((1, cols), bf16)])
 
     half, share, two_n = rows // 2, rows // parts, w_bc.shape[1]
     packed = share % 32 == 0 and rows % 128 == 0 and cols == 2 * two_n
@@ -702,12 +708,15 @@
     vecs = []
     for k in range(parts):
         theirs = lax.dynamic_slice_in_dim(in_up, adapter_of[group * seq_grp + k] * RANK, RANK, 0)
-        vecs.append(jnp.concatenate([own_vec, theirs[:, 1].astype(f32), theirs[:, 0].astype(f32)]))
-
-    first, first_labels = widened("x", jnp.concatenate([a[:, :extra] for a in along_z]), labels)
-    second, second_labels = widened("y", jnp.concatenate([a[:, extra : 2 * extra] for a in along_z]), labels)
+        vecs.append(jnp.concatenate([own_vec, theirs[:, 1], theirs[:, 0]]))
+
+    first = jnp.concatenate([a[:, :extra] for a in along_z])
+    second = jnp.concatenate([a[:, extra : 2 * extra] for a in along_z])
+    first, second, wz = lax.optimization_barrier((first, second, jnp.concatenate(wz)))
+    first, first_labels = widened("x", first, labels)
+    second, second_labels = widened("y", second, labels)
     wo, wo_labels = jnp.concatenate([a[:, 2 * extra :] for a in along_z]), labels
-    wz, wz_labels = widened("z", jnp.concatenate(wz), wz_labels)
+    wz, wz_labels = widened("z", wz, wz_labels)
     first, second, wz[1], wz[-1], wo, vecs = lax.optimization_barrier((first, second, wz[1], wz[-1], wo, jnp.stack(vecs)))
 
     vec_rows = swapped(vecs)
@@ -792,7 +801,7 @@
 
     head_sum = (head_of[:, None] == jnp.arange(heads)[None, :]).astype(bf16)
 
-    (x, w_full, bc_full, dt_full, vec, up, normed, low, pre, values, scanned, keys, prebc, scal, states) = call_scan(
+    (x, w_full, bc_full, dt_full, vec, up, normed, low, slope, values, scanned, keys, prebc, scal, states) = call_scan(
         info, gain, down_in, convbc, spread_heads,
         dict(x=x_pieces, w=x_weights, bc=bc_weights, dt=dt_weights, vec=vec_pieces),
         parts, heads, length, width, inner,
@@ -806,7 +815,7 @@
         info, normed, low, scanned, x, vec, down_out, up_out,
         dict(z=z_weights, o=o_weights, cot=cot_pieces), groups, parts,
     )
-    mixed, dlayer, dy, side, back, low_back, up_z_part, out_down_part = out
+    mixed, dlayer, dy, side, z_grad, low_back, up_z_part, out_down_part, z_full = out
 
     if mixed.ndim == 2:
         mixed = mixed.reshape(parts, groups, -1, width).transpose(1, 0, 2, 3)
@@ -814,8 +823,8 @@
     came = swapped(mixed.reshape(groups * parts, chunk, width), ("dp", "tensor"))
 
     out = call_back(
-        (x, normed, low, dlayer, dy, values, pre, keys, prebc, scal, states, scanned, side, back, low_back),
-        (w_full, bc_full, dt_full, vec, up, gain, down_in, convbc, spread_heads, head_sum)
+        (x, normed, low, dlayer, dy, values, slope, keys, prebc, scal, states, scanned, side, z_grad, low_back),
+        (w_full, z_full, bc_full, dt_full, vec, up, gain, down_in, convbc, spread_heads, head_sum)
         + (up_z_part, out_down_part), groups, parts, heads,
     )
     came, out = lax.optimization_barrier((came, out))

time: 306 us -> 301 us (0.984)
  waiting for transfers between devices: 78.2 us -> 69 us
    all_to_all x6, waiting for transfers between devices: 22.7 us -> 16.4 us  [swapped(): return lax.all_to_all(array, axes, split_axis=0, concat_axis=0, tiled=True)]
    pallas_call x1, Pallas kernels: 42.8 us -> 46.4 us  [call_back(): pl.pallas_call(functools.partial(back_kernel, groups, parts, heads), grid...]
    unnamed x92 -> x83, local copies, waits for them, and re-layouts: 6.67 us -> 5.15 us
  transfers between devices with their start and end apart: 43 -> 43, of which waited for: 15 -> 13; matrix products, arithmetic and copies ran while one was open for 10% -> 9% of each run, Pallas kernels for 28% -> 30%
where the time goes in v1:
time: 301 us; the launch traced here: 300 us
  Pallas kernels  128 us (43%)
  waiting for transfers between devices  69 us (23%)
  starting transfers between devices  63.1 us (21%)
  local copies, waits for them, and re-layouts  28.2 us (9%)
  other arithmetic  7.67 us (3%)
  between operations  4.66 us (2%)
    ppermute x36, waiting for transfers between devices, moved(): return lax.ppermute(block, axis, [(i, route(i, size)) for i in range(size)])  52.6 us
    pallas_call x1, Pallas kernels, call_back(): pl.pallas_call(functools.partial(back_kernel, groups, parts, heads), grid...  46.4 us
    ppermute x36, starting transfers between devices, moved(): return lax.ppermute(block, axis, [(i, route(i, size)) for i in range(size)])  37.2 us
    pallas_call x1, Pallas kernels, call_gate(): pl.pallas_call(functools.partial(gate_kernel, names, moves, counts), grid...  37 us
    pallas_call x1, Pallas kernels, call_scan(): pl.pallas_call(functools.partial(scan_kernel, names, moves, counts, parts...  36.9 us
    all_to_all x6, starting transfers between devices, swapped(): return lax.all_to_all(array, axes, split_axis=0, concat_axis=0, tiled=True)  24.2 us
    all_to_all x6, waiting for transfers between devices, swapped(): return lax.all_to_all(array, axes, split_axis=0, concat_axis=0, tiled=True)  16.4 us
  transfers between devices with their start and end apart: 43, of which 13 were waited for; matrix products, arithmetic and copies ran while one was open for 9% of the time, Pallas kernels for 30%

profile of v1, /device:TPU:0, one launch (start us, length us, event | category | flops | bytes accessed | tf_op | source)
XLA Modules:
  0.0 300.3 jit_solution(8532081934118463922)
XLA Ops:
  0.7 4.4 %all-to-all-start = ((bf16[4,256,1024]{2,1,0:T(8,128)(2,1)}), bf16[4,256,1024]{2,1,0:T(8,128)(2,1)S(1)}, u32[]{:S(2)}, u32[]{:S(2)}) async-start(bf16[4,256,1024]{2,1,0:T(8,128)(2,1)} %param.22), calls=%async_computation | async-start | bytes 4194304 | tf_op jit(solution)/shard_map/all_to_all | solution.py:670
  7.1 2.5 collective-permute-start
  9.6 2.6 collective-permute-start.1
  13.6 2.0 collective-permute-start.3
  20.1 13.5 %collective-permute-done.3 = bf16[1,128,512]{2,1,0:T(8,128)(2,1)S(1)} collective-permute-done((bf16[1,128,512]{2,1,0:T(8,128)(2,1)S(1)}, bf16[1,128,512]{2,1,0:T(8,128)(2,1)S(1)}, u32[]{:S(2)}, u32[]{:S(2)}) %collective-permute-start.3) | collective-permute-done | bytes 131104 | tf_op jit(solution)/shard_map/ppermute | solution.py:579
  36.0 5.3 %collective-permute-start.6 = (bf16[2,128,512]{2,1,0:T(8,128)(2,1)S(1)}, bf16[2,128,512]{2,1,0:T(8,128)(2,1)S(1)}, u32[]{:S(2)}, u32[]{:S(2)}) collective-permute-start(bf16[2,128,512]{2,1,0:T(8,128)(2,1)S(1)} %pad_maximum_fusion.6), channel_id=1, source_target_pairs={{0,8},{4,12},{8,16},{12,20},{16,24},{20,28},{24,0},{28,4},{1,9},{5... | collective-permute-start | bytes 786440 | tf_op jit(solution)/shard_map/ppermute | solution.py:579
  51.0 3.0 %collective-permute-done.7 = bf16[2,128,512]{2,1,0:T(8,128)(2,1)S(1)} collective-permute-done((bf16[2,128,512]{2,1,0:T(8,128)(2,1)S(1)}, bf16[2,128,512]{2,1,0:T(8,128)(2,1)S(1)}, u32[]{:S(2)}, u32[]{:S(2)}) %collective-permute-start.7) | collective-permute-done | bytes 262176 | tf_op jit(solution)/shard_map/ppermute | solution.py:579
  59.7 3.4 %all-to-all-start.1 = ((bf16[4,48,512]{2,1,0:T(8,128)(2,1)}), bf16[4,48,512]{2,1,0:T(8,128)(2,1)S(1)}, u32[]{:S(2)}, u32[]{:S(2)}) async-start(bf16[4,48,512]{2,1,0:T(8,128)(2,1)} %pad_maximum_fusion.8), calls=%async_computation.1 | async-start | bytes 393216 | tf_op jit(solution)/shard_map/all_to_all | solution.py:670
  68.0 5.0 %collective-permute-done.10.refs_10_ = bf16[2,128,512]{2,1,0:T(8,128)(2,1)S(1)} collective-permute-done((bf16[2,128,512]{2,1,0:T(8,128)(2,1)S(1)}, bf16[2,128,512]{2,1,0:T(8,128)(2,1)S(1)}, u32[]{:S(2)}, u32[]{:S(2)}) %collective-permute-start.10) | collective-permute-done | bytes 262176 | tf_op jit(solution)/shard_map/ppermute | solution.py:579
  73.1 2.1 all-to-all-done.1.refs_14_
  79.3 3.8 %all-to-all-start.2 = ((bf16[4,256,1024]{2,1,0:T(8,128)(2,1)}), bf16[4,256,1024]{2,1,0:T(8,128)(2,1)S(1)}, u32[]{:S(2)}, u32[]{:S(2)}) async-start(bf16[4,256,1024]{2,1,0:T(8,128)(2,1)} %param.23), calls=%async_computation.2 | async-start | bytes 4194304 | tf_op jit(solution)/shard_map/all_to_all | solution.py:670
  85.2 36.9 %shard_map.235 = (bf16[1024,1024]{1,0:T(8,128)(2,1)}, bf16[1024,2048]{1,0:T(8,128)(2,1)}, bf16[1024,256]{1,0:T(8,128)(2,1)}, bf16[32,1024]{1,0:T(8,128)(2,1)}, f...) custom-call(s32[17]{0:T(128)} %stack.116.refs_0_.info, ...), custom_call_target="tpu_custom_call" | custom-call | flops 48399998976 | bytes 1048576 | tf_op jit(solution)/shard_map/pallas_call | solution.py:236
  133.5 37.0 %shard_map.236 = (bf16[8,4,32,1024]{3,2,1,0:T(8,128)(2,1)}, bf16[1024,1024]{1,0:T(8,128)(2,1)}, bf16[1024,2048]{1,0:T(8,128)(2,1)}, bf16[1024,16]{1,0:T(8,128)(2...) custom-call(s32[17]{0:T(128)} %stack.116.refs_0_.info, ...), custom_call_target="tpu_custom_call" | custom-call | flops 47300001792 | bytes 1048576 | tf_op jit(solution)/shard_map/pallas_call | solution.py:335
  170.5 4.9 %all-to-all-start.3 = ((bf16[32,32,1024]{2,1,0:T(8,128)(2,1)}), bf16[32,32,1024]{2,1,0:T(8,128)(2,1)S(1)}, u32[]{:S(2)}, u32[]{:S(2)}) async-start(bf16[32,32,1024]{2,1,0:T(8,128)(2,1)} %bitcast.101), calls=%async_computation.3 | async-start | bytes 4194304 | tf_op jit(solution)/shard_map/all_to_all | solution.py:670
  175.5 46.4 %shard_map.237 = (bf16[1024,1024]{1,0:T(8,128)(2,1)}, bf16[32,16,256]{2,1,0:T(8,128)(2,1)}) custom-call(bf16[1024,1024]{1,0:T(8,128)(2,1)} %get-tuple-element.145.refs_4_.refs_0_, bf16[1024,1024]{1,0:T(8,128)(2,1)} %get-tuple-element.137.refs_1_, bf16[1024,16]{1,0:T(8,128)(2,1)} %get-tuple-element.143.refs_2_, ...), custom_call_target="tpu_custom_call" | custom-call | flops 54999998464 | bytes 1048576 | tf_op jit(solution)/shard_map/pallas_call | solution.py:500
  221.8 2.1 all-to-all-done.3
  224.0 4.1 %all-to-all-start.4 = ((bf16[32,16,256]{2,1,0:T(8,128)(2,1)}), bf16[32,16,256]{2,1,0:T(8,128)(2,1)S(1)}, u32[]{:S(2)}, u32[]{:S(2)}) async-start(bf16[32,16,256]{2,1,0:T(8,128)(2,1)} %get-tuple-element.177), calls=%async_computation.4 | async-start | bytes 524288 | tf_op jit(solution)/shard_map/all_to_all | solution.py:670
  228.8 9.9 %all-to-all-done.4 = bf16[32,16,256]{2,1,0:T(8,128)(2,1)S(1)} async-done(((bf16[32,16,256]{2,1,0:T(8,128)(2,1)}), bf16[32,16,256]{2,1,0:T(8,128)(2,1)S(1)}, u32[]{:S(2)}, u32[]{:S(2)}) %all-to-all-start.4) | async-done | bytes 262176 | tf_op jit(solution)/shard_map/all_to_all | solution.py:670
  242.8 3.1 %shard_map.238 = bf16[8,4,32,1024]{3,2,1,0:T(8,128)(2,1)} custom-call(s32[4]{0:T(128)} %and_select_fusion.info, bf16[8,4,32,1024]{3,2,1,0:T(8,128)(2,1)} %bitcast.100), custom_call_target="tpu_custom_call" | custom-call | flops 3300000000 | bytes 1048576 | tf_op jit(solution)/shard_map/pallas_call | solution.py:525
  247.4 3.6 %all-to-all-start.5 = ((bf16[8,4,32,1024]{3,2,1,0:T(8,128)(2,1)}), bf16[8,4,32,1024]{3,2,1,0:T(8,128)(2,1)S(1)}, u32[]{:S(2)}, u32[]{:S(2)}) async-start(bf16[8,4,32,1024]{3,2,1,0:T(8,128)(2,1)} %shard_map.238), calls=%async_computation.5 | async-start | bytes 4194304 | tf_op jit(solution)/shard_map/all_to_all | solution.py:670
  256.8 17.8 %collective-permute-done.31 = bf16[4,128,256]{2,1,0:T(8,128)(2,1)S(1)} collective-permute-done((bf16[4,128,256]{2,1,0:T(8,128)(2,1)S(1)}, bf16[4,128,256]{2,1,0:T(8,128)(2,1)S(1)}, u32[]{:S(2)}, u32[]{:S(2)}) %collective-permute-start.31) | collective-permute-done | bytes 262176 | tf_op jit(solution)/shard_map/ppermute | solution.py:579
  275.9 8.1 %collective-permute-done.32 = bf16[8,128,128]{2,1,0:T(8,128)(2,1)S(1)} collective-permute-done((bf16[8,128,128]{2,1,0:T(8,128)(2,1)S(1)}, bf16[8,128,128]{2,1,0:T(8,128)(2,1)S(1)}, u32[]{:S(2)}, u32[]{:S(2)}) %collective-permute-start.32) | collective-permute-done | bytes 262176 | tf_op jit(solution)/shard_map/ppermute | solution.py:579
  289.9 4.2 %shard_map.239 = (f32[128,1024]{1,0:T(8,128)}, f32[128,2048]{1,0:T(8,128)}, f32[128,1024]{1,0:T(8,128)}, f32[1024,128]{1,0:T(8,128)}) custom-call(s32[17]{0:T(128)} %stack.116.refs_0_.info, bf16[8,128,256]{2,1,0:T(8,128)(2,1)} %copy-done.10, bf16[16,128,128]{2,1,0:T(8,128)(2,1)} %copy-done.7, bf16[16,128,128]{2,1,0:T(8,128)(2,1)} %copy-done.30), custom_call_target="tpu_custom_call" | custom-call | flops 3300000000 | bytes 1048576 | tf_op jit(solution)/shard_map/pallas_call | solution.py:567
  296.5 2.3 all-to-all-done.5
  (212 shorter events, 67.6 us)
Async XLA Ops:
  0.7 32.9 %all-to-all-start = ((bf16[4,256,1024]{2,1,0:T(8,128)(2,1)}), bf16[4,256,1024]{2,1,0:T(8,128)(2,1)S(1)}, u32[]{:S(2)}, u32[]{:S(2)}) async-start(bf16[4,256,1024]{2,1,0:T(8,128)(2,1)} %param.22), calls=%async_computation | async-start | bytes 4194304 | tf_op jit(solution)/shard_map/all_to_all | solution.py:670
  7.1 26.5 %collective-permute-start = (bf16[1,288,512]{2,1,0:T(8,128)(2,1)S(1)}, bf16[1,288,512]{2,1,0:T(8,128)(2,1)}, u32[]{:S(2)}, u32[]{:S(2)}) collective-permute-start(bf16[1,288,512]{2,1,0:T(8,128)(2,1)S(1)} %bitcast.108), channel_id=1, source_target_pairs={{0,8},{4,12},{8,16},{12,20},{16,24},{20,28},{24,0},{28,4},{1,9},{5... | collective-permute-start | bytes 884744 | tf_op jit(solution)/shard_map/ppermute | solution.py:579
  9.6 24.0 %collective-permute-start.1 = (bf16[1,288,512]{2,1,0:T(8,128)(2,1)S(1)}, bf16[1,288,512]{2,1,0:T(8,128)(2,1)}, u32[]{:S(2)}, u32[]{:S(2)}) collective-permute-start(bf16[1,288,512]{2,1,0:T(8,128)(2,1)S(1)} %bitcast.109), channel_id=1, source_target_pairs={{0,16},{4,20},{8,24},{12,28},{16,0},{20,4},{24,8},{28,12},{1,17},{... | collective-permute-start | bytes 884744 | tf_op jit(solution)/shard_map/ppermute | solution.py:579
  12.2 21.5 %collective-permute-start.2 = (bf16[1,288,512]{2,1,0:T(8,128)(2,1)S(1)}, bf16[1,288,512]{2,1,0:T(8,128)(2,1)}, u32[]{:S(2)}, u32[]{:S(2)}) collective-permute-start(bf16[1,288,512]{2,1,0:T(8,128)(2,1)S(1)} %bitcast.110), channel_id=1, source_target_pairs={{0,24},{4,28},{8,0},{12,4},{16,8},{20,12},{24,16},{28,20},{1,25},{... | collective-permute-start | bytes 884744 | tf_op jit(solution)/shard_map/ppermute | solution.py:579
  13.6 20.1 %collective-permute-start.3 = (bf16[1,128,512]{2,1,0:T(8,128)(2,1)S(1)}, bf16[1,128,512]{2,1,0:T(8,128)(2,1)S(1)}, u32[]{:S(2)}, u32[]{:S(2)}) collective-permute-start(bf16[1,128,512]{2,1,0:T(8,128)(2,1)S(1)} %bitcast.106), channel_id=1, source_target_pairs={{0,2},{1,3},{2,0},{3,1},{4,6},{5,7},{6,4},{7,5},{8,10},{9,11},{10,... | collective-permute-start | bytes 393224 | tf_op jit(solution)/shard_map/ppermute | solution.py:579
  36.0 15.0 %collective-permute-start.6 = (bf16[2,128,512]{2,1,0:T(8,128)(2,1)S(1)}, bf16[2,128,512]{2,1,0:T(8,128)(2,1)S(1)}, u32[]{:S(2)}, u32[]{:S(2)}) collective-permute-start(bf16[2,128,512]{2,1,0:T(8,128)(2,1)S(1)} %pad_maximum_fusion.6), channel_id=1, source_target_pairs={{0,8},{4,12},{8,16},{12,20},{16,24},{20,28},{24,0},{28,4},{1,9},{5... | collective-permute-start | bytes 786440 | tf_op jit(solution)/shard_map/ppermute | solution.py:579
  54.2 21.0 %collective-permute-start.12 = (bf16[8,80,512]{2,1,0:T(8,128)(2,1)S(1)}, bf16[8,80,512]{2,1,0:T(8,128)(2,1)}, u32[]{:S(2)}, u32[]{:S(2)}) collective-permute-start(bf16[8,80,512]{2,1,0:T(8,128)(2,1)S(1)} %constant_dynamic-update-slice_fusion.5.refs_7_), channel_id=1, source_target_pairs={{0,1},{1,0},{2,3},{3,2},{4,5},{5,4},{6,7},{7,6},{8,9},{9,8},{10,11... | collective-permute-start | bytes 1966088 | tf_op jit(solution)/shard_map/ppermute | solution.py:579
  54.3 21.0 %collective-permute-start.9 = (bf16[8,80,512]{2,1,0:T(8,128)(2,1)S(1)}, bf16[8,80,512]{2,1,0:T(8,128)(2,1)}, u32[]{:S(2)}, u32[]{:S(2)}) collective-permute-start(bf16[8,80,512]{2,1,0:T(8,128)(2,1)S(1)} %constant_dynamic-update-slice_fusion.5.refs_7_), channel_id=1, source_target_pairs={{0,4},{4,0},{8,12},{12,8},{16,20},{20,16},{24,28},{28,24},{1,5},{5... | collective-permute-start | bytes 1966088 | tf_op jit(solution)/shard_map/ppermute | solution.py:579
  55.9 19.3 %collective-permute-start.11 = (bf16[8,80,512]{2,1,0:T(8,128)(2,1)S(1)}, bf16[8,80,512]{2,1,0:T(8,128)(2,1)}, u32[]{:S(2)}, u32[]{:S(2)}) collective-permute-start(bf16[8,80,512]{2,1,0:T(8,128)(2,1)S(1)} %constant_dynamic-update-slice_fusion.3.refs_6_), channel_id=1, source_target_pairs={{0,1},{1,0},{2,3},{3,2},{4,5},{5,4},{6,7},{7,6},{8,9},{9,8},{10,11... | collective-permute-start | bytes 1966088 | tf_op jit(solution)/shard_map/ppermute | solution.py:579
  56.1 19.1 %collective-permute-start.8 = (bf16[8,80,512]{2,1,0:T(8,128)(2,1)S(1)}, bf16[8,80,512]{2,1,0:T(8,128)(2,1)}, u32[]{:S(2)}, u32[]{:S(2)}) collective-permute-start(bf16[8,80,512]{2,1,0:T(8,128)(2,1)S(1)} %constant_dynamic-update-slice_fusion.3.refs_6_), channel_id=1, source_target_pairs={{0,2},{1,3},{2,0},{3,1},{4,6},{5,7},{6,4},{7,5},{8,10},{9,11},{10,... | collective-permute-start | bytes 1966088 | tf_op jit(solution)/shard_map/ppermute | solution.py:579
  58.3 14.8 %collective-permute-start.10 = (bf16[2,128,512]{2,1,0:T(8,128)(2,1)S(1)}, bf16[2,128,512]{2,1,0:T(8,128)(2,1)S(1)}, u32[]{:S(2)}, u32[]{:S(2)}) collective-permute-start(bf16[2,128,512]{2,1,0:T(8,128)(2,1)S(1)} %pad_maximum_fusion.6), channel_id=1, source_target_pairs={{0,16},{4,20},{8,24},{12,28},{16,0},{20,4},{24,8},{28,12},{1,17},{... | collective-permute-start | bytes 786440 | tf_op jit(solution)/shard_map/ppermute | solution.py:579
  59.7 15.5 %all-to-all-start.1 = ((bf16[4,48,512]{2,1,0:T(8,128)(2,1)}), bf16[4,48,512]{2,1,0:T(8,128)(2,1)S(1)}, u32[]{:S(2)}, u32[]{:S(2)}) async-start(bf16[4,48,512]{2,1,0:T(8,128)(2,1)} %pad_maximum_fusion.8), calls=%async_computation.1 | async-start | bytes 393216 | tf_op jit(solution)/shard_map/all_to_all | solution.py:670
  75.8 46.3 %collective-permute-start.17 = (bf16[4,128,512]{2,1,0:T(8,128)(2,1)}, bf16[4,128,512]{2,1,0:T(8,128)(2,1)}, u32[]{:S(2)}, u32[]{:S(2)}) collective-permute-start(bf16[4,128,512]{2,1,0:T(8,128)(2,1)} %pad_maximum_fusion.1.refs_16_), channel_id=1, source_target_pairs={{0,4},{4,0},{8,12},{12,8},{16,20},{20,16},{24,28},{28,24},{1,5},{5... | collective-permute-start | bytes 1572872 | tf_op jit(solution)/shard_map/ppermute | solution.py:579
  76.4 45.8 %collective-permute-start.18 = (bf16[4,128,512]{2,1,0:T(8,128)(2,1)}, bf16[4,128,512]{2,1,0:T(8,128)(2,1)}, u32[]{:S(2)}, u32[]{:S(2)}) collective-permute-start(bf16[4,128,512]{2,1,0:T(8,128)(2,1)} %pad_maximum_fusion.1.refs_16_), channel_id=1, source_target_pairs={{0,2},{1,3},{2,0},{3,1},{4,6},{5,7},{6,4},{7,5},{8,10},{9,11},{10,... | collective-permute-start | bytes 1572872 | tf_op jit(solution)/shard_map/ppermute | solution.py:579
  77.7 44.5 %collective-permute-start.19 = (bf16[4,128,512]{2,1,0:T(8,128)(2,1)}, bf16[4,128,512]{2,1,0:T(8,128)(2,1)}, u32[]{:S(2)}, u32[]{:S(2)}) collective-permute-start(bf16[4,128,512]{2,1,0:T(8,128)(2,1)} %pad_maximum_fusion.1.refs_16_), channel_id=1, source_target_pairs={{0,6},{1,7},{2,4},{3,5},{4,2},{5,3},{6,0},{7,1},{8,14},{9,15},{10,... | collective-permute-start | bytes 1572872 | tf_op jit(solution)/shard_map/ppermute | solution.py:790
  79.3 45.1 %all-to-all-start.2 = ((bf16[4,256,1024]{2,1,0:T(8,128)(2,1)}), bf16[4,256,1024]{2,1,0:T(8,128)(2,1)S(1)}, u32[]{:S(2)}, u32[]{:S(2)}) async-start(bf16[4,256,1024]{2,1,0:T(8,128)(2,1)} %param.23), calls=%async_computation.2 | async-start | bytes 4194304 | tf_op jit(solution)/shard_map/all_to_all | solution.py:670
  83.1 41.3 %collective-permute-start.15 = (bf16[6,128,512]{2,1,0:T(8,128)(2,1)S(1)}, bf16[6,128,512]{2,1,0:T(8,128)(2,1)}, u32[]{:S(2)}, u32[]{:S(2)}) collective-permute-start(bf16[6,128,512]{2,1,0:T(8,128)(2,1)S(1)} %copy-done.6), channel_id=1, source_target_pairs={{0,4},{4,0},{8,12},{12,8},{16,20},{20,16},{24,28},{28,24},{1,5},{5... | collective-permute-start | bytes 2359304 | tf_op jit(solution)/shard_map/ppermute | solution.py:579
  83.7 40.0 %collective-permute-start.16 = (bf16[2,128,512]{2,1,0:T(8,128)(2,1)}, bf16[2,128,512]{2,1,0:T(8,128)(2,1)S(1)}, u32[]{:S(2)}, u32[]{:S(2)}) collective-permute-start(bf16[2,128,512]{2,1,0:T(8,128)(2,1)} %copy-done.31), channel_id=1, source_target_pairs={{0,4},{4,0},{8,12},{12,8},{16,20},{20,16},{24,28},{28,24},{1,5},{5... | collective-permute-start | bytes 786440 | tf_op jit(solution)/shard_map/ppermute | solution.py:579
  170.5 53.5 %all-to-all-start.3 = ((bf16[32,32,1024]{2,1,0:T(8,128)(2,1)}), bf16[32,32,1024]{2,1,0:T(8,128)(2,1)S(1)}, u32[]{:S(2)}, u32[]{:S(2)}) async-start(bf16[32,32,1024]{2,1,0:T(8,128)(2,1)} %bitcast.101), calls=%async_computation.3 | async-start | bytes 4194304 | tf_op jit(solution)/shard_map/all_to_all | solution.py:670
  247.4 51.3 %all-to-all-start.5 = ((bf16[8,4,32,1024]{3,2,1,0:T(8,128)(2,1)}), bf16[8,4,32,1024]{3,2,1,0:T(8,128)(2,1)S(1)}, u32[]{:S(2)}, u32[]{:S(2)}) async-start(bf16[8,4,32,1024]{3,2,1,0:T(8,128)(2,1)} %shard_map.238), calls=%async_computation.5 | async-start | bytes 4194304 | tf_op jit(solution)/shard_map/all_to_all | solution.py:670
  252.8 31.3 %collective-permute-start.33 = (bf16[256,1024]{1,0:T(8,128)(2,1)S(1)}, bf16[256,1024]{1,0:T(8,128)(2,1)S(1)}, u32[]{:S(2)}, u32[]{:S(2)}) collective-permute-start(bf16[256,1024]{1,0:T(8,128)(2,1)S(1)} %get-tuple-element.208), channel_id=1, source_target_pairs={{0,1},{1,0},{2,3},{3,2},{4,5},{5,4},{6,7},{7,6},{8,9},{9,8},{10,11... | collective-permute-start | bytes 1572872 | tf_op jit(solution)/shard_map/ppermute | solution.py:579
  252.9 31.3 %collective-permute-start.34 = (bf16[256,1024]{1,0:T(8,128)(2,1)S(1)}, bf16[256,1024]{1,0:T(8,128)(2,1)S(1)}, u32[]{:S(2)}, u32[]{:S(2)}) collective-permute-start(bf16[256,1024]{1,0:T(8,128)(2,1)S(1)} %get-tuple-element.207), channel_id=1, source_target_pairs={{0,2},{1,3},{2,0},{3,1},{4,6},{5,7},{6,4},{7,5},{8,10},{9,11},{10,... | collective-permute-start | bytes 1572872 | tf_op jit(solution)/shard_map/ppermute | solution.py:579
  253.8 30.4 %collective-permute-start.35 = (bf16[256,1024]{1,0:T(8,128)(2,1)S(1)}, bf16[256,1024]{1,0:T(8,128)(2,1)S(1)}, u32[]{:S(2)}, u32[]{:S(2)}) collective-permute-start(bf16[256,1024]{1,0:T(8,128)(2,1)S(1)} %get-tuple-element.206), channel_id=1, source_target_pairs={{0,3},{1,2},{2,1},{3,0},{4,7},{5,6},{6,5},{7,4},{8,11},{9,10},{10,... | collective-permute-start | bytes 1572872 | tf_op jit(solution)/shard_map/ppermute | solution.py:579
  254.8 19.8 %collective-permute-start.31 = (bf16[4,128,256]{2,1,0:T(8,128)(2,1)S(1)}, bf16[4,128,256]{2,1,0:T(8,128)(2,1)S(1)}, u32[]{:S(2)}, u32[]{:S(2)}) collective-permute-start(bf16[4,128,256]{2,1,0:T(8,128)(2,1)S(1)} %pad_maximum_fusion.7), channel_id=1, source_target_pairs={{0,4},{4,0},{8,12},{12,8},{16,20},{20,16},{24,28},{28,24},{1,5},{5... | collective-permute-start | bytes 786440 | tf_op jit(solution)/shard_map/ppermute | solution.py:579
  (55 other events, 635.4 us)

commit v2 on v1

--- a/solution.py
+++ b/solution.py
@@ -358,7 +358,7 @@
     inner = w_full.shape[1]
     subs = ROWS // SCAN
     nstate = keys.shape[1] // 2
-    tiles = [slice(j * TILE, (j + 1) * TILE) for j in range(inner // TILE)]
+    tiles = [slice(j * 1024, (j + 1) * 1024) for j in range(inner // 1024)]
 
     @pl.when(i == 0)
     def _():
@@ -396,12 +396,12 @@
             vw = v * dtx
             dstate_low = dstate[:, cols].astype(bf16)
             within = []
-            for p in range(TILE // 128):
+            for p in range(1024 // 128):
                 part = slice(p * 128, (p + 1) * 128)
                 vw_split = split_lanes(vw[:, part])
                 lhs = []
                 for a in range(2):
-                    h = (j * TILE + p * 128) // HEAD + a
+                    h = (j * 1024 + p * 128) // HEAD + a
                     gap = cum_row[h : h + 1, :] - cum[:, h : h + 1]
                     decay = jnp.exp(jnp.minimum(gap, 0.0))
                     pulled = pulled + decay * nt(vw_split[a], g_low[:, part])
@@ -744,6 +744,8 @@
             gathered += [array] + hop("c", array)
             both_labels += [part, [dict(label, c=1) for label in part]]
             halves_of += [which, which]
+    own_cores = hop("c", wo)
+    token_rows, own_cores = lax.optimization_barrier((token_rows, own_cores))
     x_pieces = single(token_rows.reshape(length, width))
     vec_pieces = Pieces([vec_rows], [
         (0, k, None, functools.partial(lambda k, info, full: full.at[:, pl.ds(k * cols, cols)], k)) for k in range(parts)])
@@ -795,8 +797,8 @@
     def block_place(g, t, full):
         return full.at[span(g, rows), lanes(t, cols)]
 
-    def across_cores(arrays, labels):
-        arrays = arrays + [hop("c", a)[0] for a in arrays]
+    def across_cores(arrays, labels, own_core=()):
+        arrays = arrays + list(own_core) + [hop("c", a)[0] for a in arrays[len(own_core) :]]
         return placed(arrays, labels + [dict(label, c=1) for label in labels], groups, None, block_place)
 
     head_sum = (head_of[:, None] == jnp.arange(heads)[None, :]).astype(bf16)
@@ -810,7 +812,7 @@
     cot_rows = swapped(tie(cotangent, gathered[0]))
     wz, wo, cot_rows, low = lax.optimization_barrier((wz, wo, cot_rows, low))
     cot_pieces = single(cot_rows.reshape(length, width))
-    z_weights, o_weights = across_cores(wz, wz_labels), across_cores(wo, wo_labels)
+    z_weights, o_weights = across_cores(wz, wz_labels), across_cores(wo, wo_labels, own_cores)
     out = call_gate(
         info, normed, low, scanned, x, vec, down_out, up_out,
         dict(z=z_weights, o=o_weights, cot=cot_pieces), groups, parts,

time: 301 us -> 301 us (level)
  transfers between devices with their start and end apart: 43 -> 43, of which waited for: 13 -> 17; matrix products, arithmetic and copies ran while one was open for 9% -> 9% of each run, Pallas kernels for 30% -> 30%
where the time goes in v2:
time: 301 us; the launch traced here: 300 us
  Pallas kernels  127 us (42%)
  waiting for transfers between devices  70.4 us (23%)
  starting transfers between devices  62.7 us (21%)
  local copies, waits for them, and re-layouts  27.2 us (9%)
  other arithmetic  7.65 us (3%)
  between operations  4.67 us (2%)
    ppermute x36, waiting for transfers between devices, moved(): return lax.ppermute(block, axis, [(i, route(i, size)) for i in range(size)])  53.4 us
    pallas_call x1, Pallas kernels, call_back(): pl.pallas_call(functools.partial(back_kernel, groups, parts, heads), grid...  45.7 us
    ppermute x36, starting transfers between devices, moved(): return lax.ppermute(block, axis, [(i, route(i, size)) for i in range(size)])  37.1 us
    pallas_call x1, Pallas kernels, call_gate(): pl.pallas_call(functools.partial(gate_kernel, names, moves, counts), grid...  37 us
    pallas_call x1, Pallas kernels, call_scan(): pl.pallas_call(functools.partial(scan_kernel, names, moves, counts, parts...  36.9 us
    all_to_all x6, starting transfers between devices, swapped(): return lax.all_to_all(array, axes, split_axis=0, concat_axis=0, tiled=True)  24.3 us
    all_to_all x6, waiting for transfers between devices, swapped(): return lax.all_to_all(array, axes, split_axis=0, concat_axis=0, tiled=True)  17.1 us
  transfers between devices with their start and end apart: 43, of which 17 were waited for; matrix products, arithmetic and copies ran while one was open for 9% of the time, Pallas kernels for 30%

profile of v2, /device:TPU:0, one launch (start us, length us, event | category | flops | bytes accessed | tf_op | source)
XLA Modules:
  0.0 299.7 jit_solution(5607274807761263171)
XLA Ops:
  0.7 4.4 %all-to-all-start = ((bf16[4,256,1024]{2,1,0:T(8,128)(2,1)}), bf16[4,256,1024]{2,1,0:T(8,128)(2,1)S(1)}, u32[]{:S(2)}, u32[]{:S(2)}) async-start(bf16[4,256,1024]{2,1,0:T(8,128)(2,1)} %param.22), calls=%async_computation | async-start | bytes 4194304 | tf_op jit(solution)/shard_map/all_to_all | solution.py:670
  7.1 2.5 collective-permute-start
  9.6 2.6 collective-permute-start.1
  13.6 2.0 collective-permute-start.3
  20.1 13.5 %collective-permute-done.3 = bf16[1,128,512]{2,1,0:T(8,128)(2,1)S(1)} collective-permute-done((bf16[1,128,512]{2,1,0:T(8,128)(2,1)S(1)}, bf16[1,128,512]{2,1,0:T(8,128)(2,1)S(1)}, u32[]{:S(2)}, u32[]{:S(2)}) %collective-permute-start.3) | collective-permute-done | bytes 131104 | tf_op jit(solution)/shard_map/ppermute | solution.py:579
  36.0 5.3 %collective-permute-start.6 = (bf16[2,128,512]{2,1,0:T(8,128)(2,1)S(1)}, bf16[2,128,512]{2,1,0:T(8,128)(2,1)S(1)}, u32[]{:S(2)}, u32[]{:S(2)}) collective-permute-start(bf16[2,128,512]{2,1,0:T(8,128)(2,1)S(1)} %pad_maximum_fusion.6), channel_id=1, source_target_pairs={{0,8},{4,12},{8,16},{12,20},{16,24},{20,28},{24,0},{28,4},{1,9},{5... | collective-permute-start | bytes 786440 | tf_op jit(solution)/shard_map/ppermute | solution.py:579
  51.0 3.1 %collective-permute-done.7 = bf16[2,128,512]{2,1,0:T(8,128)(2,1)S(1)} collective-permute-done((bf16[2,128,512]{2,1,0:T(8,128)(2,1)S(1)}, bf16[2,128,512]{2,1,0:T(8,128)(2,1)S(1)}, u32[]{:S(2)}, u32[]{:S(2)}) %collective-permute-start.7) | collective-permute-done | bytes 262176 | tf_op jit(solution)/shard_map/ppermute | solution.py:579
  59.7 3.4 %all-to-all-start.1 = ((bf16[4,48,512]{2,1,0:T(8,128)(2,1)}), bf16[4,48,512]{2,1,0:T(8,128)(2,1)S(1)}, u32[]{:S(2)}, u32[]{:S(2)}) async-start(bf16[4,48,512]{2,1,0:T(8,128)(2,1)} %pad_maximum_fusion.8), calls=%async_computation.1 | async-start | bytes 393216 | tf_op jit(solution)/shard_map/all_to_all | solution.py:670
  68.1 5.0 %collective-permute-done.10.refs_10_ = bf16[2,128,512]{2,1,0:T(8,128)(2,1)S(1)} collective-permute-done((bf16[2,128,512]{2,1,0:T(8,128)(2,1)S(1)}, bf16[2,128,512]{2,1,0:T(8,128)(2,1)S(1)}, u32[]{:S(2)}, u32[]{:S(2)}) %collective-permute-start.10) | collective-permute-done | bytes 262176 | tf_op jit(solution)/shard_map/ppermute | solution.py:579
  73.1 2.1 all-to-all-done.1.refs_14_
  80.4 3.8 %all-to-all-start.2 = ((bf16[4,256,1024]{2,1,0:T(8,128)(2,1)}), bf16[4,256,1024]{2,1,0:T(8,128)(2,1)S(1)}, u32[]{:S(2)}, u32[]{:S(2)}) async-start(bf16[4,256,1024]{2,1,0:T(8,128)(2,1)} %param.23), calls=%async_computation.2 | async-start | bytes 4194304 | tf_op jit(solution)/shard_map/all_to_all | solution.py:670
  86.3 36.9 %shard_map.235 = (bf16[1024,1024]{1,0:T(8,128)(2,1)}, bf16[1024,2048]{1,0:T(8,128)(2,1)}, bf16[1024,256]{1,0:T(8,128)(2,1)}, bf16[32,1024]{1,0:T(8,128)(2,1)}, f...) custom-call(s32[17]{0:T(128)} %stack.116.refs_0_.info, ...), custom_call_target="tpu_custom_call" | custom-call | flops 48399998976 | bytes 1048576 | tf_op jit(solution)/shard_map/pallas_call | solution.py:236
  132.8 37.0 %shard_map.236 = (bf16[8,4,32,1024]{3,2,1,0:T(8,128)(2,1)}, bf16[1024,1024]{1,0:T(8,128)(2,1)}, bf16[1024,2048]{1,0:T(8,128)(2,1)}, bf16[1024,16]{1,0:T(8,128)(2...) custom-call(s32[17]{0:T(128)} %stack.116.refs_0_.info, ...), custom_call_target="tpu_custom_call" | custom-call | flops 47300001792 | bytes 1048576 | tf_op jit(solution)/shard_map/pallas_call | solution.py:335
  169.8 5.1 %all-to-all-start.3 = ((bf16[32,32,1024]{2,1,0:T(8,128)(2,1)}), bf16[32,32,1024]{2,1,0:T(8,128)(2,1)S(1)}, u32[]{:S(2)}, u32[]{:S(2)}) async-start(bf16[32,32,1024]{2,1,0:T(8,128)(2,1)} %bitcast.101), calls=%async_computation.3 | async-start | bytes 4194304 | tf_op jit(solution)/shard_map/all_to_all | solution.py:670
  174.9 45.7 %shard_map.237 = (bf16[1024,1024]{1,0:T(8,128)(2,1)}, bf16[32,16,256]{2,1,0:T(8,128)(2,1)}) custom-call(bf16[1024,1024]{1,0:T(8,128)(2,1)} %get-tuple-element.148.refs_4_.refs_0_, bf16[1024,1024]{1,0:T(8,128)(2,1)} %get-tuple-element.141.refs_1_, bf16[1024,16]{1,0:T(8,128)(2,1)} %get-tuple-element.146.refs_2_, ...), custom_call_target="tpu_custom_call" | custom-call | flops 54999998464 | bytes 1048576 | tf_op jit(solution)/shard_map/pallas_call | solution.py:500
  220.7 2.7 all-to-all-done.3
  223.4 4.1 %all-to-all-start.4 = ((bf16[32,16,256]{2,1,0:T(8,128)(2,1)}), bf16[32,16,256]{2,1,0:T(8,128)(2,1)S(1)}, u32[]{:S(2)}, u32[]{:S(2)}) async-start(bf16[32,16,256]{2,1,0:T(8,128)(2,1)} %get-tuple-element.181), calls=%async_computation.4 | async-start | bytes 524288 | tf_op jit(solution)/shard_map/all_to_all | solution.py:670
  228.2 9.9 %all-to-all-done.4 = bf16[32,16,256]{2,1,0:T(8,128)(2,1)S(1)} async-done(((bf16[32,16,256]{2,1,0:T(8,128)(2,1)}), bf16[32,16,256]{2,1,0:T(8,128)(2,1)S(1)}, u32[]{:S(2)}, u32[]{:S(2)}) %all-to-all-start.4) | async-done | bytes 262176 | tf_op jit(solution)/shard_map/all_to_all | solution.py:670
  242.2 3.1 %shard_map.238 = bf16[8,4,32,1024]{3,2,1,0:T(8,128)(2,1)} custom-call(s32[4]{0:T(128)} %and_select_fusion.info, bf16[8,4,32,1024]{3,2,1,0:T(8,128)(2,1)} %bitcast.100), custom_call_target="tpu_custom_call" | custom-call | flops 3300000000 | bytes 1048576 | tf_op jit(solution)/shard_map/pallas_call | solution.py:525
  246.9 3.6 %all-to-all-start.5 = ((bf16[8,4,32,1024]{3,2,1,0:T(8,128)(2,1)}), bf16[8,4,32,1024]{3,2,1,0:T(8,128)(2,1)S(1)}, u32[]{:S(2)}, u32[]{:S(2)}) async-start(bf16[8,4,32,1024]{3,2,1,0:T(8,128)(2,1)} %shard_map.238), calls=%async_computation.5 | async-start | bytes 4194304 | tf_op jit(solution)/shard_map/all_to_all | solution.py:670
  256.2 17.8 %collective-permute-done.31 = bf16[4,128,256]{2,1,0:T(8,128)(2,1)S(1)} collective-permute-done((bf16[4,128,256]{2,1,0:T(8,128)(2,1)S(1)}, bf16[4,128,256]{2,1,0:T(8,128)(2,1)S(1)}, u32[]{:S(2)}, u32[]{:S(2)}) %collective-permute-start.31) | collective-permute-done | bytes 262176 | tf_op jit(solution)/shard_map/ppermute | solution.py:579
  275.4 8.1 %collective-permute-done.32 = bf16[8,128,128]{2,1,0:T(8,128)(2,1)S(1)} collective-permute-done((bf16[8,128,128]{2,1,0:T(8,128)(2,1)S(1)}, bf16[8,128,128]{2,1,0:T(8,128)(2,1)S(1)}, u32[]{:S(2)}, u32[]{:S(2)}) %collective-permute-start.32) | collective-permute-done | bytes 262176 | tf_op jit(solution)/shard_map/ppermute | solution.py:579
  289.4 4.2 %shard_map.239 = (f32[128,1024]{1,0:T(8,128)}, f32[128,2048]{1,0:T(8,128)}, f32[128,1024]{1,0:T(8,128)}, f32[1024,128]{1,0:T(8,128)}) custom-call(s32[17]{0:T(128)} %stack.116.refs_0_.info, bf16[8,128,256]{2,1,0:T(8,128)(2,1)} %copy-done.10, bf16[16,128,128]{2,1,0:T(8,128)(2,1)} %copy-done.7, bf16[16,128,128]{2,1,0:T(8,128)(2,1)} %copy-done.30), custom_call_target="tpu_custom_call" | custom-call | flops 3300000000 | bytes 1048576 | tf_op jit(solution)/shard_map/pallas_call | solution.py:567
  295.9 2.3 all-to-all-done.5
  (210 shorter events, 66.9 us)
Async XLA Ops:
  0.7 32.9 %all-to-all-start = ((bf16[4,256,1024]{2,1,0:T(8,128)(2,1)}), bf16[4,256,1024]{2,1,0:T(8,128)(2,1)S(1)}, u32[]{:S(2)}, u32[]{:S(2)}) async-start(bf16[4,256,1024]{2,1,0:T(8,128)(2,1)} %param.22), calls=%async_computation | async-start | bytes 4194304 | tf_op jit(solution)/shard_map/all_to_all | solution.py:670
  7.1 26.5 %collective-permute-start = (bf16[1,288,512]{2,1,0:T(8,128)(2,1)S(1)}, bf16[1,288,512]{2,1,0:T(8,128)(2,1)}, u32[]{:S(2)}, u32[]{:S(2)}) collective-permute-start(bf16[1,288,512]{2,1,0:T(8,128)(2,1)S(1)} %bitcast.108), channel_id=1, source_target_pairs={{0,8},{4,12},{8,16},{12,20},{16,24},{20,28},{24,0},{28,4},{1,9},{5... | collective-permute-start | bytes 884744 | tf_op jit(solution)/shard_map/ppermute | solution.py:579
  9.6 24.0 %collective-permute-start.1 = (bf16[1,288,512]{2,1,0:T(8,128)(2,1)S(1)}, bf16[1,288,512]{2,1,0:T(8,128)(2,1)}, u32[]{:S(2)}, u32[]{:S(2)}) collective-permute-start(bf16[1,288,512]{2,1,0:T(8,128)(2,1)S(1)} %bitcast.109), channel_id=1, source_target_pairs={{0,16},{4,20},{8,24},{12,28},{16,0},{20,4},{24,8},{28,12},{1,17},{... | collective-permute-start | bytes 884744 | tf_op jit(solution)/shard_map/ppermute | solution.py:579
  12.2 21.5 %collective-permute-start.2 = (bf16[1,288,512]{2,1,0:T(8,128)(2,1)S(1)}, bf16[1,288,512]{2,1,0:T(8,128)(2,1)}, u32[]{:S(2)}, u32[]{:S(2)}) collective-permute-start(bf16[1,288,512]{2,1,0:T(8,128)(2,1)S(1)} %bitcast.110), channel_id=1, source_target_pairs={{0,24},{4,28},{8,0},{12,4},{16,8},{20,12},{24,16},{28,20},{1,25},{... | collective-permute-start | bytes 884744 | tf_op jit(solution)/shard_map/ppermute | solution.py:579
  13.6 20.1 %collective-permute-start.3 = (bf16[1,128,512]{2,1,0:T(8,128)(2,1)S(1)}, bf16[1,128,512]{2,1,0:T(8,128)(2,1)S(1)}, u32[]{:S(2)}, u32[]{:S(2)}) collective-permute-start(bf16[1,128,512]{2,1,0:T(8,128)(2,1)S(1)} %bitcast.106), channel_id=1, source_target_pairs={{0,2},{1,3},{2,0},{3,1},{4,6},{5,7},{6,4},{7,5},{8,10},{9,11},{10,... | collective-permute-start | bytes 393224 | tf_op jit(solution)/shard_map/ppermute | solution.py:579
  36.0 15.0 %collective-permute-start.6 = (bf16[2,128,512]{2,1,0:T(8,128)(2,1)S(1)}, bf16[2,128,512]{2,1,0:T(8,128)(2,1)S(1)}, u32[]{:S(2)}, u32[]{:S(2)}) collective-permute-start(bf16[2,128,512]{2,1,0:T(8,128)(2,1)S(1)} %pad_maximum_fusion.6), channel_id=1, source_target_pairs={{0,8},{4,12},{8,16},{12,20},{16,24},{20,28},{24,0},{28,4},{1,9},{5... | collective-permute-start | bytes 786440 | tf_op jit(solution)/shard_map/ppermute | solution.py:579
  54.2 21.0 %collective-permute-start.12 = (bf16[8,80,512]{2,1,0:T(8,128)(2,1)S(1)}, bf16[8,80,512]{2,1,0:T(8,128)(2,1)}, u32[]{:S(2)}, u32[]{:S(2)}) collective-permute-start(bf16[8,80,512]{2,1,0:T(8,128)(2,1)S(1)} %constant_dynamic-update-slice_fusion.5.refs_7_), channel_id=1, source_target_pairs={{0,1},{1,0},{2,3},{3,2},{4,5},{5,4},{6,7},{7,6},{8,9},{9,8},{10,11... | collective-permute-start | bytes 1966088 | tf_op jit(solution)/shard_map/ppermute | solution.py:579
  54.3 21.0 %collective-permute-start.9 = (bf16[8,80,512]{2,1,0:T(8,128)(2,1)S(1)}, bf16[8,80,512]{2,1,0:T(8,128)(2,1)}, u32[]{:S(2)}, u32[]{:S(2)}) collective-permute-start(bf16[8,80,512]{2,1,0:T(8,128)(2,1)S(1)} %constant_dynamic-update-slice_fusion.5.refs_7_), channel_id=1, source_target_pairs={{0,4},{4,0},{8,12},{12,8},{16,20},{20,16},{24,28},{28,24},{1,5},{5... | collective-permute-start | bytes 1966088 | tf_op jit(solution)/shard_map/ppermute | solution.py:579
  55.9 19.3 %collective-permute-start.11 = (bf16[8,80,512]{2,1,0:T(8,128)(2,1)S(1)}, bf16[8,80,512]{2,1,0:T(8,128)(2,1)}, u32[]{:S(2)}, u32[]{:S(2)}) collective-permute-start(bf16[8,80,512]{2,1,0:T(8,128)(2,1)S(1)} %constant_dynamic-update-slice_fusion.3.refs_6_), channel_id=1, source_target_pairs={{0,1},{1,0},{2,3},{3,2},{4,5},{5,4},{6,7},{7,6},{8,9},{9,8},{10,11... | collective-permute-start | bytes 1966088 | tf_op jit(solution)/shard_map/ppermute | solution.py:579
  56.1 19.1 %collective-permute-start.8 = (bf16[8,80,512]{2,1,0:T(8,128)(2,1)S(1)}, bf16[8,80,512]{2,1,0:T(8,128)(2,1)}, u32[]{:S(2)}, u32[]{:S(2)}) collective-permute-start(bf16[8,80,512]{2,1,0:T(8,128)(2,1)S(1)} %constant_dynamic-update-slice_fusion.3.refs_6_), channel_id=1, source_target_pairs={{0,2},{1,3},{2,0},{3,1},{4,6},{5,7},{6,4},{7,5},{8,10},{9,11},{10,... | collective-permute-start | bytes 1966088 | tf_op jit(solution)/shard_map/ppermute | solution.py:579
  58.3 14.8 %collective-permute-start.10 = (bf16[2,128,512]{2,1,0:T(8,128)(2,1)S(1)}, bf16[2,128,512]{2,1,0:T(8,128)(2,1)S(1)}, u32[]{:S(2)}, u32[]{:S(2)}) collective-permute-start(bf16[2,128,512]{2,1,0:T(8,128)(2,1)S(1)} %pad_maximum_fusion.6), channel_id=1, source_target_pairs={{0,16},{4,20},{8,24},{12,28},{16,0},{20,4},{24,8},{28,12},{1,17},{... | collective-permute-start | bytes 786440 | tf_op jit(solution)/shard_map/ppermute | solution.py:579
  59.7 15.5 %all-to-all-start.1 = ((bf16[4,48,512]{2,1,0:T(8,128)(2,1)}), bf16[4,48,512]{2,1,0:T(8,128)(2,1)S(1)}, u32[]{:S(2)}, u32[]{:S(2)}) async-start(bf16[4,48,512]{2,1,0:T(8,128)(2,1)} %pad_maximum_fusion.8), calls=%async_computation.1 | async-start | bytes 393216 | tf_op jit(solution)/shard_map/all_to_all | solution.py:670
  75.9 47.3 %collective-permute-start.18 = (bf16[4,128,512]{2,1,0:T(8,128)(2,1)}, bf16[4,128,512]{2,1,0:T(8,128)(2,1)}, u32[]{:S(2)}, u32[]{:S(2)}) collective-permute-start(bf16[4,128,512]{2,1,0:T(8,128)(2,1)} %pad_maximum_fusion.1.refs_16_), channel_id=1, source_target_pairs={{0,4},{4,0},{8,12},{12,8},{16,20},{20,16},{24,28},{28,24},{1,5},{5... | collective-permute-start | bytes 1572872 | tf_op jit(solution)/shard_map/ppermute | solution.py:579
  76.4 46.8 %collective-permute-start.19 = (bf16[4,128,512]{2,1,0:T(8,128)(2,1)}, bf16[4,128,512]{2,1,0:T(8,128)(2,1)}, u32[]{:S(2)}, u32[]{:S(2)}) collective-permute-start(bf16[4,128,512]{2,1,0:T(8,128)(2,1)} %pad_maximum_fusion.1.refs_16_), channel_id=1, source_target_pairs={{0,2},{1,3},{2,0},{3,1},{4,6},{5,7},{6,4},{7,5},{8,10},{9,11},{10,... | collective-permute-start | bytes 1572872 | tf_op jit(solution)/shard_map/ppermute | solution.py:579
  79.1 44.1 %collective-permute-start.20 = (bf16[4,128,512]{2,1,0:T(8,128)(2,1)}, bf16[4,128,512]{2,1,0:T(8,128)(2,1)}, u32[]{:S(2)}, u32[]{:S(2)}) collective-permute-start(bf16[4,128,512]{2,1,0:T(8,128)(2,1)} %pad_maximum_fusion.1.refs_16_), channel_id=1, source_target_pairs={{0,6},{1,7},{2,4},{3,5},{4,2},{5,3},{6,0},{7,1},{8,14},{9,15},{10,... | collective-permute-start | bytes 1572872 | tf_op jit(solution)/shard_map/ppermute | solution.py:792
  80.4 44.4 %all-to-all-start.2 = ((bf16[4,256,1024]{2,1,0:T(8,128)(2,1)}), bf16[4,256,1024]{2,1,0:T(8,128)(2,1)S(1)}, u32[]{:S(2)}, u32[]{:S(2)}) async-start(bf16[4,256,1024]{2,1,0:T(8,128)(2,1)} %param.23), calls=%async_computation.2 | async-start | bytes 4194304 | tf_op jit(solution)/shard_map/all_to_all | solution.py:670
  84.3 40.6 %collective-permute-start.16 = (bf16[6,128,512]{2,1,0:T(8,128)(2,1)S(1)}, bf16[6,128,512]{2,1,0:T(8,128)(2,1)}, u32[]{:S(2)}, u32[]{:S(2)}) collective-permute-start(bf16[6,128,512]{2,1,0:T(8,128)(2,1)S(1)} %copy-done.6), channel_id=1, source_target_pairs={{0,4},{4,0},{8,12},{12,8},{16,20},{20,16},{24,28},{28,24},{1,5},{5... | collective-permute-start | bytes 2359304 | tf_op jit(solution)/shard_map/ppermute | solution.py:579
  85.8 38.3 %collective-permute-start.17 = (bf16[2,128,512]{2,1,0:T(8,128)(2,1)}, bf16[2,128,512]{2,1,0:T(8,128)(2,1)S(1)}, u32[]{:S(2)}, u32[]{:S(2)}) collective-permute-start(bf16[2,128,512]{2,1,0:T(8,128)(2,1)} %copy-done.31), channel_id=1, source_target_pairs={{0,4},{4,0},{8,12},{12,8},{16,20},{20,16},{24,28},{28,24},{1,5},{5... | collective-permute-start | bytes 786440 | tf_op jit(solution)/shard_map/ppermute | solution.py:579
  169.8 53.6 %all-to-all-start.3 = ((bf16[32,32,1024]{2,1,0:T(8,128)(2,1)}), bf16[32,32,1024]{2,1,0:T(8,128)(2,1)S(1)}, u32[]{:S(2)}, u32[]{:S(2)}) async-start(bf16[32,32,1024]{2,1,0:T(8,128)(2,1)} %bitcast.101), calls=%async_computation.3 | async-start | bytes 4194304 | tf_op jit(solution)/shard_map/all_to_all | solution.py:670
  246.9 51.3 %all-to-all-start.5 = ((bf16[8,4,32,1024]{3,2,1,0:T(8,128)(2,1)}), bf16[8,4,32,1024]{3,2,1,0:T(8,128)(2,1)S(1)}, u32[]{:S(2)}, u32[]{:S(2)}) async-start(bf16[8,4,32,1024]{3,2,1,0:T(8,128)(2,1)} %shard_map.238), calls=%async_computation.5 | async-start | bytes 4194304 | tf_op jit(solution)/shard_map/all_to_all | solution.py:670
  252.2 31.3 %collective-permute-start.33 = (bf16[256,1024]{1,0:T(8,128)(2,1)S(1)}, bf16[256,1024]{1,0:T(8,128)(2,1)S(1)}, u32[]{:S(2)}, u32[]{:S(2)}) collective-permute-start(bf16[256,1024]{1,0:T(8,128)(2,1)S(1)} %get-tuple-element.212), channel_id=1, source_target_pairs={{0,1},{1,0},{2,3},{3,2},{4,5},{5,4},{6,7},{7,6},{8,9},{9,8},{10,11... | collective-permute-start | bytes 1572872 | tf_op jit(solution)/shard_map/ppermute | solution.py:579
  252.3 31.3 %collective-permute-start.34 = (bf16[256,1024]{1,0:T(8,128)(2,1)S(1)}, bf16[256,1024]{1,0:T(8,128)(2,1)S(1)}, u32[]{:S(2)}, u32[]{:S(2)}) collective-permute-start(bf16[256,1024]{1,0:T(8,128)(2,1)S(1)} %get-tuple-element.211), channel_id=1, source_target_pairs={{0,2},{1,3},{2,0},{3,1},{4,6},{5,7},{6,4},{7,5},{8,10},{9,11},{10,... | collective-permute-start | bytes 1572872 | tf_op jit(solution)/shard_map/ppermute | solution.py:579
  253.2 30.4 %collective-permute-start.35 = (bf16[256,1024]{1,0:T(8,128)(2,1)S(1)}, bf16[256,1024]{1,0:T(8,128)(2,1)S(1)}, u32[]{:S(2)}, u32[]{:S(2)}) collective-permute-start(bf16[256,1024]{1,0:T(8,128)(2,1)S(1)} %get-tuple-element.210), channel_id=1, source_target_pairs={{0,3},{1,2},{2,1},{3,0},{4,7},{5,6},{6,5},{7,4},{8,11},{9,10},{10,... | collective-permute-start | bytes 1572872 | tf_op jit(solution)/shard_map/ppermute | solution.py:579
  254.2 19.8 %collective-permute-start.31 = (bf16[4,128,256]{2,1,0:T(8,128)(2,1)S(1)}, bf16[4,128,256]{2,1,0:T(8,128)(2,1)S(1)}, u32[]{:S(2)}, u32[]{:S(2)}) collective-permute-start(bf16[4,128,256]{2,1,0:T(8,128)(2,1)S(1)} %pad_maximum_fusion.7), channel_id=1, source_target_pairs={{0,4},{4,0},{8,12},{12,8},{16,20},{20,16},{24,28},{28,24},{1,5},{5... | collective-permute-start | bytes 786440 | tf_op jit(solution)/shard_map/ppermute | solution.py:579
  (54 other events, 635.1 us)
